TPU v7x, 128 devices: a whole 4x4x4 slice. The times are simulated.
128 devices in a mesh: row: 8 (over y, core), col: 16 (over z, x).
Axes of the slice: x: 4, y: 4, z: 4, core: 2. Of those that a mesh axis runs over, the one named last changes fastest.
Arguments:
- shell_velocity: bfloat16 [1024, 128, 128], P(('row', 'col')), may hold values from -6 to 6
- coupling: bfloat16 [1024, 2, 2, 256, 128], P(('row', 'col')), may hold values from -0.375 to 0.375
- coupling_dest: int32 [1024, 2], P(('row', 'col')), may hold values from 0 to 15, all different within a row; in each aligned block of 8 rows (0 to 7, 8 to 15, ...) at most 2 rows name the same one
- coupling_cluster: int32 [1024, 2], P(('row', 'col')), may hold values from 0 to 63
- near_blocks: bfloat16 [8, 16, 32, 2, 256, 256], P('row', 'col'), may hold values from -0.046875 to 0.046875
- far_v: bfloat16 [8, 16, 64, 2, 32, 256], P('row', 'col'), may hold values from -0.25 to 0.25
- far_u: bfloat16 [8, 16, 64, 2, 32, 256], P('row', 'col'), may hold values from -0.09375 to 0.09375
- block_pairs: int32 [8, 16, 96], P('row', 'col'), may hold values from 0 to 1023, as said below
Outputs:
- response: bfloat16 [32768, 128], P(('row', 'col'))
Inputs may be any that keep to these rules, and one draw needn't show every extreme that they name: `coupling_dest`: the rows of one device name any column group at most 2 times, and some device names one exactly 2 times; the 2 entries of a row differ. `block_pairs`: each entry codes a row cluster r and column cluster c of its group as r * 64 + c; the entries of one group are distinct.
All inputs are finite; a program needn't handle non-finite values.
Results may differ from a plain program's by a relative error of at most 0.008.
Values may be sent and summed in bfloat16 or wider, within the bound.
No kernel may reach another device: no remote copies, remote signals or barrier semaphores. Data moves between devices by JAX's collectives and lax.ppermute only.
A program may use at most 128 MiB of HBM per device.

v0:
```python
import jax
import jax.numpy as jnp
from jax import lax
from jax.sharding import PartitionSpec as P

RC_DEV = 16
CC_DEV = 64
NEAR_DEV = 32


def rotate_blocks(values, load_count):
    return jnp.concatenate([-values[..., load_count:], values[..., :load_count]], axis=-1)


def per_device(
    shell_velocity,
    coupling,
    coupling_dest,
    coupling_cluster,
    near_blocks,
    far_v,
    far_u,
    block_pairs,
):
    width = shell_velocity.shape[-1]
    load_count = width // 2
    shell_count = shell_velocity.shape[0]
    top_count = coupling.shape[1]
    panels = coupling.shape[3]
    contributions = jnp.einsum(
        "stpq,sqk->stpk", coupling[:, :, 0], shell_velocity, preferred_element_type=jnp.float32
    )
    contributions = contributions + jnp.einsum(
        "stpq,sqk->stpk",
        coupling[:, :, 1],
        rotate_blocks(shell_velocity, load_count),
        preferred_element_type=jnp.float32,
    )
    entries = shell_count * top_count
    flat_rows = contributions.astype(jnp.bfloat16).reshape(entries, panels * width)
    col_count = lax.axis_size("col")
    capacity = max(2, (entries + col_count - 1) // col_count)
    target = coupling_dest.reshape(entries)
    target_cluster = coupling_cluster.reshape(entries)
    onehot = (target[:, None] == jnp.arange(col_count, dtype=jnp.int32)[None, :]).astype(jnp.int32)
    before = jnp.cumsum(onehot, axis=0) - onehot
    slot_rank = jnp.sum(before * onehot, axis=1)
    slot_index = target * capacity + slot_rank
    slot_pick = jnp.arange(col_count * capacity, dtype=jnp.int32)[:, None] == slot_index[None, :]
    outgoing = jnp.dot(
        slot_pick.astype(jnp.bfloat16), flat_rows, preferred_element_type=jnp.float32
    )
    outgoing = outgoing.astype(jnp.bfloat16).reshape(col_count, capacity, panels, width)
    slot_ids = jnp.sum(slot_pick.astype(jnp.int32) * (target_cluster + 1)[None, :], axis=1) - 1
    slot_ids = slot_ids.reshape(col_count, capacity)
    incoming, got_ids = (
        lax.all_to_all(outgoing, "col", split_axis=0, concat_axis=0, tiled=True),
        lax.all_to_all(slot_ids, "col", split_axis=0, concat_axis=0, tiled=True),
    )
    cluster_pick = (
        jnp.arange(CC_DEV, dtype=jnp.int32)[:, None] == got_ids.reshape(-1)[None, :]
    ).astype(jnp.bfloat16)
    cluster_sums = jnp.dot(
        cluster_pick,
        incoming.reshape(col_count * capacity, panels * width),
        preferred_element_type=jnp.float32,
    ).reshape(CC_DEV, panels, width)
    sources = lax.psum(cluster_sums, "row").astype(jnp.bfloat16)
    pair_codes = block_pairs.reshape(-1)
    owners = pair_codes // CC_DEV
    columns = pair_codes % CC_DEV
    nearby_local = near_blocks[0, 0]
    nearby_input = sources[columns[:NEAR_DEV]]
    nearby_contribution = jnp.einsum(
        "dym,dmg->dyg", nearby_local[:, 0], nearby_input, preferred_element_type=jnp.float32
    )
    nearby_contribution = nearby_contribution + jnp.einsum(
        "dym,dmg->dyg",
        nearby_local[:, 1],
        rotate_blocks(nearby_input, load_count),
        preferred_element_type=jnp.float32,
    )
    distant_input = sources[columns[NEAR_DEV:]]
    distant_right_factor = far_v[0, 0]
    expansion_coefficients = jnp.einsum(
        "dyz,dzi->dyi",
        distant_right_factor[:, 0],
        distant_input,
        preferred_element_type=jnp.float32,
    )
    expansion_coefficients = expansion_coefficients + jnp.einsum(
        "dyz,dzi->dyi",
        distant_right_factor[:, 1],
        rotate_blocks(distant_input, load_count),
        preferred_element_type=jnp.float32,
    )
    expansion_coefficients = expansion_coefficients.astype(jnp.bfloat16)
    far_left = far_u[0, 0]
    far_term = jnp.einsum(
        "brp,brk->bpk", far_left[:, 0], expansion_coefficients, preferred_element_type=jnp.float32
    )
    far_term = far_term + jnp.einsum(
        "brp,brk->bpk",
        far_left[:, 1],
        rotate_blocks(expansion_coefficients, load_count),
        preferred_element_type=jnp.float32,
    )
    all_terms = jnp.concatenate([nearby_contribution, far_term], axis=0)
    high_part = all_terms.astype(jnp.bfloat16)
    low_part = (all_terms - high_part.astype(jnp.float32)).astype(jnp.bfloat16)
    owner_pick = (jnp.arange(RC_DEV, dtype=jnp.int32)[:, None] == owners[None, :]).astype(
        jnp.bfloat16
    )
    row_sums = jnp.einsum("ib,bpk->ipk", owner_pick, high_part, preferred_element_type=jnp.float32)
    row_sums = row_sums + jnp.einsum(
        "ib,bpk->ipk", owner_pick, low_part, preferred_element_type=jnp.float32
    )
    row_sums = row_sums.reshape(RC_DEV * panels, width)
    return lax.psum_scatter(row_sums, "col", scatter_dimension=0, tiled=True).astype(jnp.bfloat16)


def solution(mesh):
    return jax.shard_map(
        per_device,
        mesh=mesh,
        in_specs=(
            P(("row", "col"), None, None),
            P(("row", "col"), None, None, None, None),
            P(("row", "col"), None),
            P(("row", "col"), None),
            P("row", "col", None, None, None, None),
            P("row", "col", None, None, None, None),
            P("row", "col", None, None, None, None),
            P("row", "col", None),
        ),
        out_specs=P(("row", "col"), None),
        check_vma=False,
    )
```

profile of v0, /device:TPU:0, one launch (start us, length us, event | category | flops | bytes accessed | tf_op | source)
XLA Modules:
  0.0 325.1 jit_solution(17533050063739755453)
XLA Ops:
  9.5 8.0 %all-to-all-start = ((s32[16,1,2]{2,1,0:T(1,128)}), s32[16,1,2]{2,1,0:T(1,128)S(1)}, u32[]{:S(2)}, u32[]{:S(2)}) async-start(s32[16,1,2]{2,1,0:T(1,128)} %bitcast.2), calls=%async_computation | async-start | bytes 16384 | tf_op jit(solution)/shard_map/all_to_all | solution.py:58
  17.4 1.2 fusion.46
  18.9 1.7 fusion.20
  22.0 1.8 copy.96
  24.9 6.1 %all-to-all-start.1 = ((bf16[16,2,256,128]{3,2,1,0:T(8,128)(2,1)}), bf16[16,2,256,128]{3,2,1,0:T(8,128)(2,1)S(1)}, u32[]{:S(2)}, u32[]{:S(2)}) async-start(bf16[16,2,256,128]{3,2,1,0:T(8,128)(2,1)} %bitcast.38), calls=%async_computation.1 | async-start | bytes 4194304 | tf_op jit(solution)/shard_map/all_to_all | solution.py:57
  31.1 3.3 %copy.114 = bf16[1,1,64,2,32,256]{5,4,2,3,1,0:T(8,128)(2,1)} copy(bf16[1,1,64,2,32,256]{5,4,3,2,1,0:T(8,128)(2,1)} %param.13) | data formatting | bytes 4194304 | tf_op args[5]
  34.4 1.5 copy.113
  35.9 7.7 %copy.112 = bf16[1,1,32,2,256,256]{5,4,2,3,1,0:T(8,128)(2,1)} copy(bf16[1,1,32,2,256,256]{5,4,3,2,1,0:T(8,128)(2,1)} %param.12) | data formatting | bytes 16777216 | tf_op args[4]
  44.9 16.4 %all-to-all-done.1 = bf16[16,2,256,128]{3,2,1,0:T(8,128)(2,1)S(1)} async-done(((bf16[16,2,256,128]{3,2,1,0:T(8,128)(2,1)}), bf16[16,2,256,128]{3,2,1,0:T(8,128)(2,1)S(1)}, u32[]{:S(2)}, u32[]{:S(2)}) %all-to-all-start.1) | async-done | bytes 2097184 | tf_op jit(solution)/shard_map/all_to_all | solution.py:57
  61.3 4.8 %fusion.7 = f32[64,256,128]{2,0,1:T(8,128)} fusion(s32[32]{0:T(128)S(1)} %eq.66, bf16[4,8,256,128]{3,2,1,0:T(8,128)(2,1)S(1)} %bitcast.117), kind=kOutput, calls=%fused_computation.19 | convolution fusion | flops 134219776 | bytes 10485888 | tf_op jit(solution)/shard_map/dot_general | solution.py:63
  66.1 90.6 %all-reduce.1 = bf16[64,256,128]{2,0,1:T(8,128)(2,1)} all-reduce(f32[64,256,128]{2,0,1:T(8,128)} %fusion.7), channel_id=1, replica_groups=mesh['row'=8,'col'=16] {'row'}, use_global_device_ids=true, to_apply=%region_3.4 | all-reduce | flops 2097152 | bytes 12582912 | tf_op jit(solution)/shard_map/psum | solution.py:68
  156.7 6.8 %copy.73 = bf16[64,256,128]{2,1,0:T(8,128)(2,1)} copy(bf16[64,256,128]{2,0,1:T(8,128)(2,1)} %all-reduce.1) | data formatting | bytes 8388608 | tf_op jit(solution)/shard_map/convert_element_type | solution.py:68
  163.5 3.1 gather_fusion
  166.7 5.2 %gather_fusion.1 = bf16[64,256,128]{2,1,0:T(8,128)(2,1)} fusion(bf16[64,256,128]{2,1,0:T(8,128)(2,1)} %copy.73, s32[1024]{0:T(1024)S(1)} %pad_clamp_fusion), kind=kCustom, calls=%fused_computation.1 | custom fusion | bytes 8388864 | tf_op jit(solution)/shard_map/gather | solution.py:83
  171.9 2.8 fusion.45
  174.7 1.9 copy.92
  176.6 1.2 neg.13
  177.8 1.9 copy.93
  179.8 4.0 %fusion.1 = f32[32,128,256]{2,1,0:T(8,128)S(1)} fusion(bf16[32,2,256,256]{3,2,0,1:T(8,128)(2,1)} %bitcast.110, bf16[32,256,64]{1,2,0:T(8,128)(2,1)S(1)} %copy.93, bf16[32,256,64]{1,2,0:T(8,128)(2,1)} %neg.13), kind=kOutput, calls=%fused_computation.10 | convolution fusion | flops 541065216 | bytes 10485760 | tf_op jit(solution)/shard_map/dym,dmg->dyg/dot_general | solution.py:77
  183.8 5.8 %add_bitcast_fusion.1 = f32[32,256,128]{1,2,0:T(8,128)} fusion(f32[32,128,256]{2,1,0:T(8,128)S(1)} %fusion.1, bf16[32,256,128]{2,1,0:T(8,128)(2,1)S(1)} %gather_fusion, bf16[32,2,256,256]{3,2,0,1:T(8,128)(2,1)} %bitcast.111), kind=kOutput, calls=%fused_computation.17 | convolution fusion | flops 537919488 | bytes 14680064 | tf_op jit(solution)/shard_map/dym,dmg->dyg/dot_general | solution.py:74
  189.6 2.0 slice_negate_fusion
  191.6 2.3 fusion.3
  195.5 1.3 fusion.18
  196.8 5.1 %add_bitcast_fusion = f32[64,256,128]{1,2,0:T(8,128)} fusion(f32[64,128,256]{2,1,0:T(8,128)S(1)} %fusion.18, bf16[64,2,32,256]{3,2,0,1:T(8,128)(2,1)S(1)} %bitcast.113, bf16[64,32,64]{2,1,0:T(8,128)(2,1)S(1)} %get-tuple-element.10, bf16[64,32,64]{2,1,0:T(8,128)(2,1)S(1)} %get-tuple-element.9), kind=kOutput, calls=%fused_computation.7 | convolution fusion | flops 137363456 | bytes 18874368 | tf_op jit(solution)/shard_map/brp,brk->bpk/dot_general | solution.py:102
  201.9 9.0 %subtract_convert_fusion = bf16[96,256,128]{1,2,0:T(8,128)(2,1)} fusion(f32[64,256,128]{1,2,0:T(8,128)} %add_bitcast_fusion, f32[32,256,128]{1,2,0:T(8,128)} %add_bitcast_fusion.1), kind=kLoop, calls=%fused_computation.4 | loop fusion | flops 15728640 | bytes 18874368 | tf_op jit(solution)/shard_map/convert_element_type | solution.py:110
  210.9 7.9 %fusion = bf16[96,256,128]{1,2,0:T(8,128)(2,1)} fusion(f32[64,256,128]{1,2,0:T(8,128)} %add_bitcast_fusion, f32[32,256,128]{1,2,0:T(8,128)} %add_bitcast_fusion.1), kind=kLoop, calls=%fused_computation.5 | loop fusion | flops 3145728 | bytes 18874368 | tf_op jit(solution)/shard_map/convert_element_type | solution.py:109
  218.8 9.1 %copy.81 = bf16[96,256,128]{2,0,1:T(8,128)(2,1)} copy(bf16[96,256,128]{1,2,0:T(8,128)(2,1)} %fusion) | data formatting | bytes 12582912 | tf_op jit(solution)/shard_map/convert_element_type | solution.py:109
  228.0 9.1 %copy.82 = bf16[96,256,128]{2,0,1:T(8,128)(2,1)} copy(bf16[96,256,128]{1,2,0:T(8,128)(2,1)} %subtract_convert_fusion) | data formatting | bytes 12582912 | tf_op jit(solution)/shard_map/convert_element_type | solution.py:110
  237.0 3.9 %fusion.36 = f32[16,256,128]{2,0,1:T(8,128)S(1)} fusion(bf16[96,256,128]{2,0,1:T(8,128)(2,1)} %copy.81, s32[96]{0:T(128)S(1)} %get-tuple-element.13), kind=kOutput, calls=%fused_computation.63 | convolution fusion | flops 100664832 | bytes 8388992 | tf_op jit(solution)/shard_map/ib,bpk->ipk/dot_general | solution.py:114
  242.6 2.0 copy.83
  244.6 72.1 %reduce-scatter.2.cloned.1.call-done = f32[256,128]{1,0:T(8,128)} async-done(((f32[4096,128]{1,0:T(8,128)}), f32[256,128]{1,0:T(8,128)}) %reduce-scatter.2.cloned.1.call-update) | async-done | bytes 131088 | tf_op jit(solution)/shard_map/reduce_scatter | solution.py:119
  316.7 1.5 convert_element_type.43
  (45 shorter events, 10.4 us)
Async XLA Ops:
  6.5 14.1 %copy-start.4 = (bf16[8,2,2,256,128]{4,3,2,1,0:T(8,128)(2,1)S(1)}, bf16[8,2,2,256,128]{4,3,2,1,0:T(8,128)(2,1)}, u32[]{:S(2)}) copy-start(bf16[8,2,2,256,128]{4,3,2,1,0:T(8,128)(2,1)} %param.9) | copy-start | bytes 6291460
  9.5 15.4 %all-to-all-start = ((s32[16,1,2]{2,1,0:T(1,128)}), s32[16,1,2]{2,1,0:T(1,128)S(1)}, u32[]{:S(2)}, u32[]{:S(2)}) async-start(s32[16,1,2]{2,1,0:T(1,128)} %bitcast.2), calls=%async_computation | async-start | bytes 16384 | tf_op jit(solution)/shard_map/all_to_all | solution.py:58
  24.9 36.4 %all-to-all-start.1 = ((bf16[16,2,256,128]{3,2,1,0:T(8,128)(2,1)}), bf16[16,2,256,128]{3,2,1,0:T(8,128)(2,1)S(1)}, u32[]{:S(2)}, u32[]{:S(2)}) async-start(bf16[16,2,256,128]{3,2,1,0:T(8,128)(2,1)} %bitcast.38), calls=%async_computation.1 | async-start | bytes 4194304 | tf_op jit(solution)/shard_map/all_to_all | solution.py:57
  31.0 285.7 %reduce-scatter.2.cloned.1.call-start = ((), (), s32[]{:S(2)}) async-start(), calls=%async_computation.3 | async-start | bytes 2228224 | tf_op jit(solution)/shard_map/reduce_scatter | solution.py:119
  31.1 3.3 %copy-start.5 = (bf16[1,1,64,2,32,256]{5,4,3,2,1,0:T(8,128)(2,1)S(1)}, bf16[1,1,64,2,32,256]{5,4,3,2,1,0:T(8,128)(2,1)}, u32[]{:S(2)}) copy-start(bf16[1,1,64,2,32,256]{5,4,3,2,1,0:T(8,128)(2,1)} %param.14) | copy-start | bytes 6291460
  35.9 7.7 %copy-start.6 = (s32[1,1,96]{2,1,0:T(1,128)S(1)}, s32[1,1,96]{2,1,0:T(1,128)}, u32[]{:S(2)}) copy-start(s32[1,1,96]{2,1,0:T(1,128)} %param.15) | copy-start | bytes 1156
  183.8 5.8 %copy-start = (bf16[64,256,128]{2,1,0:T(8,128)(2,1)S(1)}, bf16[64,256,128]{2,1,0:T(8,128)(2,1)}, u32[]{:S(2)}) copy-start(bf16[64,256,128]{2,1,0:T(8,128)(2,1)} %gather_fusion.1) | copy-start | bytes 12582916
  189.6 2.0 copy-start.3
  193.9 1.6 copy-start.2
  237.0 4.6 %copy-start.1 = (bf16[96,256,128]{2,0,1:T(8,128)(2,1)S(1)}, bf16[96,256,128]{2,0,1:T(8,128)(2,1)}, u32[]{:S(2)}) copy-start(bf16[96,256,128]{2,0,1:T(8,128)(2,1)} %copy.82) | copy-start | bytes 18874372
Sparse Core Ops, SparseCore 0:
  244.7 71.9 reduce-scatter.1
where the time goes:
time: 326 us; the launch traced here: 325 us
  blocking collectives  90.6 us (28%)
  waiting for transfers between devices  89.6 us (27%)
  local copies, waits for them, and re-layouts  61.3 us (19%)
  matrix products  32 us (10%)
  other arithmetic  23.9 us (7%)
  starting transfers between devices  14.1 us (4%)
  between operations  13.6 us (4%)
    psum x1, blocking collectives, per_device(): sources = lax.psum(cluster_sums, 'row').astype(jnp.bfloat16)  90.6 us
    reduce_scatter x1, waiting for transfers between devices, per_device(): lax.psum_scatter(row_sums, 'col', scatter_dimension=0, tiled=True)  72.1 us
    unnamed x23, local copies, waits for them, and re-layouts  20.4 us
    all_to_all x1, waiting for transfers between devices, per_device(): lax.all_to_all(outgoing, 'col', split_axis=0, concat_axis=0, tiled=True)  16.4 us
    convert_element_type x1, local copies, waits for them, and re-layouts, per_device(): high_part = all_terms.astype(jnp.bfloat16)  9.13 us
    convert_element_type x1, local copies, waits for them, and re-layouts, per_device(): low_part = (all_terms - high_part.astype(jnp.float32)).astype(jnp.bfloat16)  9.09 us
    convert_element_type x1, other arithmetic, per_device(): low_part = (all_terms - high_part.astype(jnp.float32)).astype(jnp.bfloat16)  8.97 us
    all_to_all x1, starting transfers between devices, per_device(): lax.all_to_all(slot_ids, 'col', split_axis=0, concat_axis=0, tiled=True)  7.96 us
  transfers between devices with their start and end apart: 3, of which 3 were waited for; matrix products, arithmetic and copies ran while one was open for 6% of the time, Pallas kernels for 0%

commit v1 on v0

v1 whole, which is shorter than its diff:
```python
import jax
import jax.numpy as jnp
from jax import lax
from jax.experimental import pallas as pl
from jax.experimental.pallas import tpu as pltpu
from jax.sharding import PartitionSpec as P

LOADS = 64
WIDTH = 128
PANELS = 256
SHELL_DEV = 8
TOP = 2
ROWS = 8
COLS = 16
CLUSTERS = 64
NEAR = 32
FAR = 64
SLOTS = 2
PIECE = WIDTH // ROWS
DATA = SLOTS * 2 * PIECE
MESSAGE = DATA + 8
NEAR_STEP = 4
FAR_STEP = 8
STEPS = NEAR // NEAR_STEP
VMEM_LIMIT = 40 * 1024 * 1024

F32 = jnp.float32
BF16 = jnp.bfloat16


def dot_t(a, b):
    return lax.dot_general(a, b, (((1,), (1,)), ((), ())), preferred_element_type=F32)


def dot_n(a, b):
    return lax.dot_general(a, b, (((1,), (0,)), ((), ())), preferred_element_type=F32)


def rotate_rows(values):
    half = values.shape[0] // 2
    return jnp.concatenate([-values[half:], values[:half]], axis=0)


def contribution_kernel(dest_ref, cluster_ref, velocity_ref, coupling_ref, out_ref, count_ref, ids_ref):
    step = pl.program_id(0)

    @pl.when(step == 0)
    def _():
        for h in range(COLS):
            count_ref[h] = 0
            ids_ref[2 * h] = CLUSTERS
            ids_ref[2 * h + 1] = CLUSTERS

    velocity = velocity_ref[0].astype(F32).T
    wide = jnp.concatenate([velocity, rotate_rows(velocity)], axis=1).astype(BF16)
    for t in range(TOP):
        h = dest_ref[step, t]
        slot = jnp.minimum(count_ref[h], SLOTS - 1)
        count_ref[h] = slot + 1
        ids_ref[2 * h + slot] = cluster_ref[step, t]
        blocks = jnp.concatenate([coupling_ref[0, t, 0], coupling_ref[0, t, 1]], axis=1)
        product = dot_t(wide, blocks).astype(BF16)
        start = pl.multiple_of(slot * (2 * PIECE), 2 * PIECE)
        for r in range(ROWS):
            for half in range(2):
                out_ref[r, h, pl.ds(start + half * PIECE, PIECE), :] = product[
                    r * PIECE : (r + 1) * PIECE, half * 128 : (half + 1) * 128
                ]

    @pl.when(step == SHELL_DEV - 1)
    def _():
        me = lax.axis_index("row") * COLS + lax.axis_index("col")
        row = lax.broadcasted_iota(jnp.int32, (8, 128), 0)
        lane = lax.broadcasted_iota(jnp.int32, (8, 128), 1)
        place = row * 128 + lane
        for h in range(COLS):
            tile = jnp.where(place == 2 * me, ids_ref[2 * h], 0)
            tile = jnp.where(place == 2 * me + 1, ids_ref[2 * h + 1], tile)
            tile = tile.astype(F32).astype(BF16)
            for r in range(ROWS):
                out_ref[r, h, DATA:MESSAGE, :] = tile


def contributions(dest, cluster, velocity, coupling):
    return pl.pallas_call(
        contribution_kernel,
        grid=(SHELL_DEV,),
        out_shape=jax.ShapeDtypeStruct((ROWS, COLS, MESSAGE, 128), BF16),
        in_specs=[
            pl.BlockSpec(memory_space=pltpu.SMEM),
            pl.BlockSpec(memory_space=pltpu.SMEM),
            pl.BlockSpec((1, 128, WIDTH), lambda s: (s, 0, 0)),
            pl.BlockSpec((1, TOP, 2, PANELS, 128), lambda s: (s, 0, 0, 0, 0)),
        ],
        out_specs=pl.BlockSpec((ROWS, COLS, MESSAGE, 128), lambda s: (0, 0, 0, 0)),
        scratch_shapes=[pltpu.SMEM((COLS,), jnp.int32), pltpu.SMEM((2 * COLS,), jnp.int32)],
        compiler_params=pltpu.CompilerParams(vmem_limit_bytes=VMEM_LIMIT),
        name="contributions",
    )(dest, cluster, velocity, coupling)


def cluster_kernel(got_ref, out_ref, total_ref, ids_vec_ref, ids_ref, sem):
    devices = got_ref.shape[0]
    ids = jnp.zeros((8, 128), F32)
    for s in range(devices):
        ids = ids + got_ref[s, DATA:MESSAGE, :].astype(F32)
    ids_vec_ref[...] = ids.astype(jnp.int32)
    copy = pltpu.make_async_copy(ids_vec_ref, ids_ref, sem)
    copy.start()
    total_ref[...] = jnp.zeros_like(total_ref)
    copy.wait()

    def add(s, carry):
        for slot in range(SLOTS):
            k = ids_ref[s // 64, 2 * (s % 64) + slot]
            piece = got_ref[s, slot * 2 * PIECE : (slot + 1) * 2 * PIECE, :]
            total_ref[k] = total_ref[k] + piece.astype(F32)
        return carry

    lax.fori_loop(0, devices, add, 0, unroll=8)
    out_ref[...] = total_ref[:CLUSTERS].astype(BF16)


def cluster_sums(got):
    return pl.pallas_call(
        cluster_kernel,
        out_shape=jax.ShapeDtypeStruct((CLUSTERS, 2 * PIECE, 128), BF16),
        in_specs=[pl.BlockSpec(memory_space=pltpu.VMEM)],
        out_specs=pl.BlockSpec(memory_space=pltpu.VMEM),
        scratch_shapes=[
            pltpu.VMEM((CLUSTERS + 1, 2 * PIECE, 128), F32),
            pltpu.VMEM((8, 128), jnp.int32),
            pltpu.SMEM((8, 128), jnp.int32),
            pltpu.SemaphoreType.DMA,
        ],
        compiler_params=pltpu.CompilerParams(vmem_limit_bytes=VMEM_LIMIT),
        name="cluster_sums",
    )(got)


def shift_rows(values, pairs):
    return lax.ppermute(values, "row", pairs)


def gather_pieces(own):
    half = CLUSTERS // 2
    up = [(s, (s + 2) % ROWS) for s in range(ROWS)]
    down = [(s, (s - 2) % ROWS) for s in range(ROWS)]
    twin = [(s, s ^ 1) for s in range(ROWS)]
    below = shift_rows(own, up)
    above = shift_rows(own, down)
    far_low = shift_rows(below[:half], up)
    far_high = shift_rows(above[half:], down)
    pieces = [(own, 0, 0), (below, 0, 3), (above, 0, 1), (far_low, 0, 2), (far_high, half, 2)]
    result = []
    for values, first, offset in pieces:
        result.append((values, first, offset, 0))
        result.append((shift_rows(values, twin), first, offset, 1))
    return result


def operator_kernel(places, pairs_ref, *refs):
    count = len(places)
    piece_refs = refs[:count]
    near_ref, right_ref, left_ref, out_ref, source_ref, total_ref, sem = refs[count:]
    step = pl.program_id(0)

    @pl.when(step == 0)
    def _():
        me = lax.axis_index("row")
        copies = []
        for i, (first, size, offset, core) in enumerate(places):
            row = ((me // 2 + offset) % 4) * 2 + (me + core) % 2
            start = pl.multiple_of(row * PIECE, PIECE)
            for part in range(2):
                copies.append(
                    pltpu.make_async_copy(
                        piece_refs[i].at[:, pl.ds(part * PIECE, PIECE), :],
                        source_ref.at[pl.ds(first, size), pl.ds(start, PIECE), pl.ds(part * 128, 128)],
                        sem.at[2 * i + part],
                    )
                )
        for copy in copies:
            copy.start()
        total_ref[...] = jnp.zeros_like(total_ref)
        for copy in copies:
            copy.wait()

    def sources(place):
        code = pairs_ref[place]
        values = source_ref[code % CLUSTERS]
        return code // CLUSTERS, jnp.concatenate([values, rotate_rows(values)], axis=1)

    for j in range(NEAR_STEP):
        owner, wide = sources(step * NEAR_STEP + j)
        blocks = jnp.concatenate([near_ref[j, 0], near_ref[j, 1]], axis=1)
        total_ref[owner] = total_ref[owner] + dot_t(wide, blocks)
    for j in range(FAR_STEP):
        owner, wide = sources(NEAR + step * FAR_STEP + j)
        right = jnp.concatenate([right_ref[j, 0], right_ref[j, 1]], axis=1)
        coeffs = dot_t(wide, right).astype(BF16)
        term = dot_n(coeffs, left_ref[j, 0]) + dot_n(rotate_rows(coeffs), left_ref[j, 1])
        total_ref[owner] = total_ref[owner] + term

    @pl.when(step == STEPS - 1)
    def _():
        out_ref[...] = total_ref[...].astype(BF16)


def apply_operator(pairs, pieces, near, right, left):
    places = [(first, values.shape[0], offset, core) for values, first, offset, core in pieces]

    def kernel(*refs):
        operator_kernel(places, *refs)

    return pl.pallas_call(
        kernel,
        grid=(STEPS,),
        out_shape=jax.ShapeDtypeStruct((COLS, WIDTH, PANELS), BF16),
        in_specs=[pl.BlockSpec(memory_space=pltpu.SMEM)]
        + [pl.BlockSpec(memory_space=pl.ANY)] * len(pieces)
        + [
            pl.BlockSpec((NEAR_STEP, 2, PANELS, PANELS), lambda s: (s, 0, 0, 0)),
            pl.BlockSpec((FAR_STEP, 2, 32, PANELS), lambda s: (s, 0, 0, 0)),
            pl.BlockSpec((FAR_STEP, 2, 32, PANELS), lambda s: (s, 0, 0, 0)),
        ],
        out_specs=pl.BlockSpec((COLS, WIDTH, PANELS), lambda s: (0, 0, 0)),
        scratch_shapes=[
            pltpu.VMEM((CLUSTERS, WIDTH, PANELS), BF16),
            pltpu.VMEM((COLS, WIDTH, PANELS), F32),
            pltpu.SemaphoreType.DMA((2 * len(pieces),)),
        ],
        compiler_params=pltpu.CompilerParams(vmem_limit_bytes=VMEM_LIMIT),
        name="operator",
    )(pairs, *[piece[0] for piece in pieces], near, right, left)


def response_kernel(got_ref, out_ref):
    total = got_ref[0].astype(F32)
    for i in range(1, COLS):
        total = total + got_ref[i].astype(F32)
    out_ref[...] = total.T.astype(BF16)


def response_sum(got):
    return pl.pallas_call(
        response_kernel,
        out_shape=jax.ShapeDtypeStruct((PANELS, WIDTH), BF16),
        in_specs=[pl.BlockSpec(memory_space=pltpu.VMEM)],
        out_specs=pl.BlockSpec(memory_space=pltpu.VMEM),
        compiler_params=pltpu.CompilerParams(vmem_limit_bytes=VMEM_LIMIT),
        name="response_sum",
    )(got)


def per_device(velocity, coupling, dest, cluster, near, far_v, far_u, pairs):
    messages = contributions(dest, cluster, velocity, coupling)
    messages = messages.reshape(ROWS * COLS, MESSAGE, 128)
    got = lax.all_to_all(messages, ("row", "col"), split_axis=0, concat_axis=0, tiled=True)
    own = cluster_sums(got)
    pieces = gather_pieces(own)
    partial = apply_operator(pairs.reshape(-1), pieces, near[0, 0], far_v[0, 0], far_u[0, 0])
    gathered = lax.all_to_all(partial, "col", split_axis=0, concat_axis=0, tiled=True)
    return response_sum(gathered)


def solution(mesh):
    return jax.shard_map(
        per_device,
        mesh=mesh,
        in_specs=(
            P(("row", "col"), None, None),
            P(("row", "col"), None, None, None, None),
            P(("row", "col"), None),
            P(("row", "col"), None),
            P("row", "col", None, None, None, None),
            P("row", "col", None, None, None, None),
            P("row", "col", None, None, None, None),
            P("row", "col", None),
        ),
        out_specs=P(("row", "col"), None),
        check_vma=False,
    )
```

time: 326 us -> 113 us (0.35)
  waiting for transfers between devices: 89.6 us -> 19.7 us
  local copies, waits for them, and re-layouts: 61.3 us -> 4.09 us
  matrix products: 32 us -> 0 us
  blocking collectives: 90.6 us -> 65.1 us
  other arithmetic: 23.9 us -> 0 us
  Pallas kernels: 0 us -> 18.4 us
  between operations: 13.6 us -> 0.09 us
  starting transfers between devices: 14.1 us -> 5.4 us
    psum x1 -> x0, blocking collectives: 90.6 us -> none  [per_device(): sources = lax.psum(cluster_sums, 'row').astype(jnp.bfloat16)]
    reduce_scatter x1 -> x0, waiting for transfers between devices: 72.1 us -> none  [per_device(): lax.psum_scatter(row_sums, 'col', scatter_dimension=0, tiled=True)]
    all_to_all x0 -> x2, blocking collectives: none -> 65.1 us  [the longest x1 43.3 us: per_device(): lax.all_to_all(messages, ('row', 'col'), split_axis=0, concat_axis=0, til...]
    dot_general x12 -> x0, matrix products: 32 us -> none  [the longest x1 5.79 us: per_device(): jnp.einsum('dym,dmg->dyg', nearby_local[:, 0], nearby_input, preferred_el...]
    convert_element_type x3 -> x0, local copies, waits for them, and re-layouts: 25 us -> none  [the longest x1 9.13 us: per_device(): high_part = all_terms.astype(jnp.bfloat16)]
    ppermute x0 -> x9, waiting for transfers between devices: none -> 19.7 us  [shift_rows(): return lax.ppermute(values, 'row', pairs)]
    convert_element_type x4 -> x0, other arithmetic: 18.5 us -> none  [the longest x1 8.97 us: per_device(): low_part = (all_terms - high_part.astype(jnp.float32)).astype(jnp.bfloat16)]
    pallas_call x0 -> x4, Pallas kernels: none -> 18.4 us  [the longest x1 12.3 us: apply_operator(): pl.pallas_call(kernel, grid=(STEPS,), out_shape=jax.ShapeDtypeStruct((COL...]
  transfers between devices with their start and end apart: 3 -> 9, of which waited for: 3 -> 4; matrix products, arithmetic and copies ran while one was open for 6% -> 0% of each run, Pallas kernels for 0% -> 0%
where the time goes in v1:
time: 113 us
  blocking collectives  65.1 us (58%)
  waiting for transfers between devices  19.7 us (17%)
  Pallas kernels  18.4 us (16%)
  starting transfers between devices  5.4 us (5%)
  local copies, waits for them, and re-layouts  4.09 us (4%)
    all_to_all x1, blocking collectives, per_device(): lax.all_to_all(messages, ('row', 'col'), split_axis=0, concat_axis=0, til...  43.3 us
    all_to_all x1, blocking collectives, per_device(): lax.all_to_all(partial, 'col', split_axis=0, concat_axis=0, tiled=True)  21.8 us
    ppermute x9, waiting for transfers between devices, shift_rows(): return lax.ppermute(values, 'row', pairs)  19.7 us
    pallas_call x1, Pallas kernels, apply_operator(): pl.pallas_call(kernel, grid=(STEPS,), out_shape=jax.ShapeDtypeStruct((COL...  12.3 us
    ppermute x9, starting transfers between devices, shift_rows(): return lax.ppermute(values, 'row', pairs)  5.4 us
    unnamed x12, local copies, waits for them, and re-layouts  4.06 us
    pallas_call x1, Pallas kernels, contributions(): pl.pallas_call(contribution_kernel, grid=(SHELL_DEV,), out_shape=jax.Shap...  2.9 us
    pallas_call x1, Pallas kernels, cluster_sums(): pl.pallas_call(cluster_kernel, out_shape=jax.ShapeDtypeStruct((CLUSTERS,...  2.32 us
  transfers between devices with their start and end apart: 9, of which 4 were waited for; matrix products, arithmetic and copies ran while one was open for 0% of the time, Pallas kernels for 0%

profile of v1, /device:TPU:0, one launch (start us, length us, event | category | flops | bytes accessed | tf_op | source)
XLA Modules:
  0.0 112.7 jit_solution(4519982726093266652)
XLA Ops:
  0.0 0.8 copy.9.dest_ref
  0.8 0.8 copy.10.cluster_ref
  1.5 1.6 %copy-done.2 = bf16[8,2,2,256,128]{4,3,2,1,0:T(8,128)(2,1)S(1)} copy-done((bf16[8,2,2,256,128]{4,3,2,1,0:T(8,128)(2,1)S(1)}, bf16[8,2,2,256,128]{4,3,2,1,0:T(8,128)(2,1)}, u32[]{:S(2)}) %copy-start.2) | copy-done | bytes 2097176
  3.1 0.9 copy-done.3
  4.0 2.9 %contributions.1 = bf16[8,16,72,128]{3,2,1,0:T(8,128)(2,1)S(1)} custom-call(s32[8,2]{1,0:T(8,128)S(1)} %copy.9.dest_ref, s32[8,2]{1,0:T(8,128)S(1)} %copy.10.cluster_ref, bf16[8,128,128]{2,1,0:T(8,128)(2,1)S(1)} %copy-done.3, bf16[8,2,2,256,128]{4,3,2,1,0:T(8,128)(2,1)S(1)} %copy-done.2), custom_call_target="tpu_custom_call" | custom-call | tf_op jit(solution)/shard_map/contributions/pallas_call | solution.py:85
  7.0 0.0 copy-start.1
  7.0 43.3 %all_to_all.10.got_ref = bf16[128,72,128]{2,1,0:T(8,128)(2,1)S(1)} all-to-all(bf16[128,72,128]{2,1,0:T(8,128)(2,1)S(1)} %bitcast.5), channel_id=1, replica_groups=mesh['row'=8,'col'=16] {'row','col'}, dimensions={0} | all-to-all | bytes 4718592 | tf_op jit(solution)/shard_map/all_to_all | solution.py:259
  50.3 2.3 %cluster_sums.1.refs_1_ = bf16[64,32,128]{2,1,0:T(8,128)(2,1)S(1)} custom-call(bf16[128,72,128]{2,1,0:T(8,128)(2,1)S(1)} %all_to_all.10.got_ref), custom_call_target="tpu_custom_call" | custom-call | tf_op jit(solution)/shard_map/cluster_sums/pallas_call | solution.py:125
  52.6 1.3 %collective-permute-start.3 = (bf16[64,32,128]{2,1,0:T(8,128)(2,1)S(1)}, bf16[64,32,128]{2,1,0:T(8,128)(2,1)S(1)}, u32[]{:S(2)}, u32[]{:S(2)}) collective-permute-start(bf16[64,32,128]{2,1,0:T(8,128)(2,1)S(1)} %cluster_sums.1.refs_1_), channel_id=1, source_target_pairs={{0,96},{16,112},{32,0},{48,16},{64,32},{80,48},{96,64},{112,80},{1... | collective-permute-start | bytes 1572872 | tf_op jit(solution)/shard_map/ppermute | solution.py:142
  53.9 0.8 collective-permute-start.1
  54.7 0.0 collective-permute-start
  54.7 11.1 %collective-permute-done.3.refs_5_ = bf16[64,32,128]{2,1,0:T(8,128)(2,1)S(1)} collective-permute-done((bf16[64,32,128]{2,1,0:T(8,128)(2,1)S(1)}, bf16[64,32,128]{2,1,0:T(8,128)(2,1)S(1)}, u32[]{:S(2)}, u32[]{:S(2)}) %collective-permute-start.3) | collective-permute-done | bytes 524320 | tf_op jit(solution)/shard_map/ppermute | solution.py:142
  65.8 2.6 %collective-permute-start.7 = (bf16[32,32,128]{2,1,0:T(8,128)(2,1)S(1)}, bf16[32,32,128]{2,1,0:T(8,128)(2,1)S(1)}, u32[]{:S(2)}, u32[]{:S(2)}) collective-permute-start(bf16[32,32,128]{2,1,0:T(8,128)(2,1)S(1)} %slice.9), channel_id=1, source_target_pairs={{0,96},{16,112},{32,0},{48,16},{64,32},{80,48},{96,64},{112,80},{1... | collective-permute-start | bytes 786440 | tf_op jit(solution)/shard_map/ppermute | solution.py:142
  68.5 0.0 collective-permute-done.1.refs_3_
  68.5 0.1 collective-permute-start.5
  68.6 0.1 collective-permute-start.4
  68.7 0.5 collective-permute-start.2
  69.2 3.5 %collective-permute-done.7.refs_9_ = bf16[32,32,128]{2,1,0:T(8,128)(2,1)S(1)} collective-permute-done((bf16[32,32,128]{2,1,0:T(8,128)(2,1)S(1)}, bf16[32,32,128]{2,1,0:T(8,128)(2,1)S(1)}, u32[]{:S(2)}, u32[]{:S(2)}) %collective-permute-start.7) | collective-permute-done | bytes 262176 | tf_op jit(solution)/shard_map/ppermute | solution.py:142
  72.7 0.0 collective-permute-start.8
  72.7 3.5 %collective-permute-done.5.refs_7_ = bf16[32,32,128]{2,1,0:T(8,128)(2,1)S(1)} collective-permute-done((bf16[32,32,128]{2,1,0:T(8,128)(2,1)S(1)}, bf16[32,32,128]{2,1,0:T(8,128)(2,1)S(1)}, u32[]{:S(2)}, u32[]{:S(2)}) %collective-permute-start.5) | collective-permute-done | bytes 262176 | tf_op jit(solution)/shard_map/ppermute | solution.py:142
  76.2 0.0 collective-permute-start.6
  76.2 0.0 collective-permute-done.refs_2_
  76.2 0.0 collective-permute-done.8.refs_10_
  76.2 0.0 collective-permute-done.4.refs_6_
  76.2 1.5 %collective-permute-done.6.refs_8_ = bf16[32,32,128]{2,1,0:T(8,128)(2,1)S(1)} collective-permute-done((bf16[32,32,128]{2,1,0:T(8,128)(2,1)S(1)}, bf16[32,32,128]{2,1,0:T(8,128)(2,1)S(1)}, u32[]{:S(2)}, u32[]{:S(2)}) %collective-permute-start.6) | collective-permute-done | bytes 262176 | tf_op jit(solution)/shard_map/ppermute | solution.py:142
  77.7 0.0 collective-permute-done.2.refs_4_
  77.7 0.0 copy-done.1
  77.7 0.0 copy-done
  77.8 0.0 copy-done.4
  77.8 12.3 %operator.1 = bf16[16,128,256]{2,1,0:T(8,128)(2,1)S(1)} custom-call(s32[96]{0:T(128)S(1)} %bitcast.8, bf16[64,32,128]{2,1,0:T(8,128)(2,1)S(1)} %cluster_sums.1.refs_1_, bf16[64,32,128]{2,1,0:T(8,128)(2,1)S(1)} %collective-permute-done.refs_2_, bf16[64,32,128]{2,1,0:T(8,128)(2,1)S(1)} %collective-permute-done.1.refs_3_, ...), custom_call_target="tpu_custom_call" | custom-call | tf_op jit(solution)/shard_map/operator/pallas_call | solution.py:216
  90.1 21.8 %all_to_all.11.got_ref = bf16[16,128,256]{2,1,0:T(8,128)(2,1)S(1)} all-to-all(bf16[16,128,256]{2,1,0:T(8,128)(2,1)S(1)} %operator.1), channel_id=1, replica_groups=mesh['row'=8,'col'=16] {'col'}, dimensions={0} | all-to-all | bytes 2097152 | tf_op jit(solution)/shard_map/all_to_all | solution.py:263
  111.9 0.8 response_sum.1
  (6 shorter events, 0.0 us)
Async XLA Ops:
  1.5 1.6 %copy-start.2 = (bf16[8,2,2,256,128]{4,3,2,1,0:T(8,128)(2,1)S(1)}, bf16[8,2,2,256,128]{4,3,2,1,0:T(8,128)(2,1)}, u32[]{:S(2)}) copy-start(bf16[8,2,2,256,128]{4,3,2,1,0:T(8,128)(2,1)} %coupling_ref.1) | copy-start | bytes 6291460
  3.1 0.9 copy-start.3
  7.0 70.8 %copy-start.1 = (bf16[1,1,64,2,32,256]{5,4,3,2,1,0:T(8,128)(2,1)S(1)}, bf16[1,1,64,2,32,256]{5,4,3,2,1,0:T(8,128)(2,1)}, u32[]{:S(2)}) copy-start(bf16[1,1,64,2,32,256]{5,4,3,2,1,0:T(8,128)(2,1)} %param.14) | copy-start | bytes 6291460
  50.3 27.5 %copy-start = (bf16[1,1,64,2,32,256]{5,4,3,2,1,0:T(8,128)(2,1)S(1)}, bf16[1,1,64,2,32,256]{5,4,3,2,1,0:T(8,128)(2,1)}, u32[]{:S(2)}) copy-start(bf16[1,1,64,2,32,256]{5,4,3,2,1,0:T(8,128)(2,1)} %param.13) | copy-start | bytes 6291460
  50.3 27.5 %copy-start.4 = (s32[1,1,96]{2,1,0:T(1,128)S(1)}, s32[1,1,96]{2,1,0:T(1,128)}, u32[]{:S(2)}) copy-start(s32[1,1,96]{2,1,0:T(1,128)} %param.15) | copy-start | bytes 1156
  52.6 13.2 %collective-permute-start.3 = (bf16[64,32,128]{2,1,0:T(8,128)(2,1)S(1)}, bf16[64,32,128]{2,1,0:T(8,128)(2,1)S(1)}, u32[]{:S(2)}, u32[]{:S(2)}) collective-permute-start(bf16[64,32,128]{2,1,0:T(8,128)(2,1)S(1)} %cluster_sums.1.refs_1_), channel_id=1, source_target_pairs={{0,96},{16,112},{32,0},{48,16},{64,32},{80,48},{96,64},{112,80},{1... | collective-permute-start | bytes 1572872 | tf_op jit(solution)/shard_map/ppermute | solution.py:142
  53.9 14.5 %collective-permute-start.1 = (bf16[64,32,128]{2,1,0:T(8,128)(2,1)S(1)}, bf16[64,32,128]{2,1,0:T(8,128)(2,1)S(1)}, u32[]{:S(2)}, u32[]{:S(2)}) collective-permute-start(bf16[64,32,128]{2,1,0:T(8,128)(2,1)S(1)} %cluster_sums.1.refs_1_), channel_id=1, source_target_pairs={{0,32},{16,48},{32,64},{48,80},{64,96},{80,112},{96,0},{112,16},{1... | collective-permute-start | bytes 1572872 | tf_op jit(solution)/shard_map/ppermute | solution.py:142
  54.7 21.5 %collective-permute-start = (bf16[64,32,128]{2,1,0:T(8,128)(2,1)S(1)}, bf16[64,32,128]{2,1,0:T(8,128)(2,1)S(1)}, u32[]{:S(2)}, u32[]{:S(2)}) collective-permute-start(bf16[64,32,128]{2,1,0:T(8,128)(2,1)S(1)} %cluster_sums.1.refs_1_), channel_id=1, source_target_pairs={{0,16},{16,0},{32,48},{48,32},{64,80},{80,64},{96,112},{112,96},{1... | collective-permute-start | bytes 1572872 | tf_op jit(solution)/shard_map/ppermute | solution.py:142
  65.8 6.9 %collective-permute-start.7 = (bf16[32,32,128]{2,1,0:T(8,128)(2,1)S(1)}, bf16[32,32,128]{2,1,0:T(8,128)(2,1)S(1)}, u32[]{:S(2)}, u32[]{:S(2)}) collective-permute-start(bf16[32,32,128]{2,1,0:T(8,128)(2,1)S(1)} %slice.9), channel_id=1, source_target_pairs={{0,96},{16,112},{32,0},{48,16},{64,32},{80,48},{96,64},{112,80},{1... | collective-permute-start | bytes 786440 | tf_op jit(solution)/shard_map/ppermute | solution.py:142
  68.5 7.7 %collective-permute-start.5 = (bf16[32,32,128]{2,1,0:T(8,128)(2,1)S(1)}, bf16[32,32,128]{2,1,0:T(8,128)(2,1)S(1)}, u32[]{:S(2)}, u32[]{:S(2)}) collective-permute-start(bf16[32,32,128]{2,1,0:T(8,128)(2,1)S(1)} %slice.8), channel_id=1, source_target_pairs={{0,32},{16,48},{32,64},{48,80},{64,96},{80,112},{96,0},{112,16},{1... | collective-permute-start | bytes 786440 | tf_op jit(solution)/shard_map/ppermute | solution.py:142
  68.6 7.6 %collective-permute-start.4 = (bf16[64,32,128]{2,1,0:T(8,128)(2,1)S(1)}, bf16[64,32,128]{2,1,0:T(8,128)(2,1)S(1)}, u32[]{:S(2)}, u32[]{:S(2)}) collective-permute-start(bf16[64,32,128]{2,1,0:T(8,128)(2,1)S(1)} %collective-permute-done.3.refs_5_), channel_id=1, source_target_pairs={{0,16},{16,0},{32,48},{48,32},{64,80},{80,64},{96,112},{112,96},{1... | collective-permute-start | bytes 1572872 | tf_op jit(solution)/shard_map/ppermute | solution.py:142
  68.7 9.1 %collective-permute-start.2 = (bf16[64,32,128]{2,1,0:T(8,128)(2,1)S(1)}, bf16[64,32,128]{2,1,0:T(8,128)(2,1)S(1)}, u32[]{:S(2)}, u32[]{:S(2)}) collective-permute-start(bf16[64,32,128]{2,1,0:T(8,128)(2,1)S(1)} %collective-permute-done.1.refs_3_), channel_id=1, source_target_pairs={{0,16},{16,0},{32,48},{48,32},{64,80},{80,64},{96,112},{112,96},{1... | collective-permute-start | bytes 1572872 | tf_op jit(solution)/shard_map/ppermute | solution.py:142
  72.7 3.5 %collective-permute-start.8 = (bf16[32,32,128]{2,1,0:T(8,128)(2,1)S(1)}, bf16[32,32,128]{2,1,0:T(8,128)(2,1)S(1)}, u32[]{:S(2)}, u32[]{:S(2)}) collective-permute-start(bf16[32,32,128]{2,1,0:T(8,128)(2,1)S(1)} %collective-permute-done.7.refs_9_), channel_id=1, source_target_pairs={{0,16},{16,0},{32,48},{48,32},{64,80},{80,64},{96,112},{112,96},{1... | collective-permute-start | bytes 786440 | tf_op jit(solution)/shard_map/ppermute | solution.py:142
  76.2 1.5 %collective-permute-start.6 = (bf16[32,32,128]{2,1,0:T(8,128)(2,1)S(1)}, bf16[32,32,128]{2,1,0:T(8,128)(2,1)S(1)}, u32[]{:S(2)}, u32[]{:S(2)}) collective-permute-start(bf16[32,32,128]{2,1,0:T(8,128)(2,1)S(1)} %collective-permute-done.5.refs_7_), channel_id=1, source_target_pairs={{0,16},{16,0},{32,48},{48,32},{64,80},{80,64},{96,112},{112,96},{1... | collective-permute-start | bytes 786440 | tf_op jit(solution)/shard_map/ppermute | solution.py:142

commit v2 on v1

v2 whole, which is shorter than its diff:
```python
import jax
import jax.numpy as jnp
from jax import lax
from jax.experimental import pallas as pl
from jax.experimental.pallas import tpu as pltpu
from jax.sharding import PartitionSpec as P

LOADS = 64
WIDTH = 128
PANELS = 256
SHELL_DEV = 8
TOP = 2
ROWS = 8
COLS = 16
CLUSTERS = 64
NEAR = 32
FAR = 64
SLOTS = 2
PIECE = WIDTH // ROWS
DATA = SLOTS * 2 * PIECE
MESSAGE = DATA + 8
NEAR_STEP = 8
FAR_STEP = 16
RANK = 32
STEPS = NEAR // NEAR_STEP
VMEM_LIMIT = 12 * 1024 * 1024
FIRST_LIMIT = 54 * 1024 * 1024

F32 = jnp.float32
BF16 = jnp.bfloat16


def dot_t(a, b):
    return lax.dot_general(a, b, (((1,), (1,)), ((), ())), preferred_element_type=F32)


def dot_n(a, b):
    return lax.dot_general(a, b, (((1,), (0,)), ((), ())), preferred_element_type=F32)


def rotate_rows(values):
    half = values.shape[0] // 2
    return jnp.concatenate([-values[half:], values[:half]], axis=0)


def contribution_kernel(
    dest_ref, cluster_ref, velocity_hbm, coupling_hbm, out_ref, count_ref, ids_ref, velocity_ref, coupling_ref, sem
):
    velocity_copy = pltpu.make_async_copy(velocity_hbm, velocity_ref, sem.at[SHELL_DEV])
    copies = [
        pltpu.make_async_copy(coupling_hbm.at[s], coupling_ref.at[s], sem.at[s]) for s in range(SHELL_DEV)
    ]
    velocity_copy.start()
    for copy in copies:
        copy.start()
    for h in range(COLS):
        count_ref[h] = 0
        ids_ref[2 * h] = CLUSTERS
        ids_ref[2 * h + 1] = CLUSTERS
    velocity_copy.wait()
    for s in range(SHELL_DEV):
        velocity = velocity_ref[s].astype(F32).T
        wide = jnp.concatenate([velocity, rotate_rows(velocity)], axis=1).astype(BF16)
        copies[s].wait()
        for t in range(TOP):
            h = dest_ref[t, s]
            slot = jnp.minimum(count_ref[h], SLOTS - 1)
            count_ref[h] = slot + 1
            ids_ref[2 * h + slot] = cluster_ref[t, s]
            blocks = jnp.concatenate([coupling_ref[s, t, 0], coupling_ref[s, t, 1]], axis=1)
            product = dot_t(wide, blocks).astype(BF16)
            start = pl.multiple_of(slot * (2 * PIECE), 2 * PIECE)
            for r in range(ROWS):
                first = (r % 2) * LOADS + (r // 2) * PIECE
                for half in range(2):
                    out_ref[r, h, pl.ds(start + half * PIECE, PIECE), :] = product[
                        first : first + PIECE, half * 128 : (half + 1) * 128
                    ]
    me = lax.axis_index("row") * COLS + lax.axis_index("col")
    row = lax.broadcasted_iota(jnp.int32, (8, 128), 0)
    lane = lax.broadcasted_iota(jnp.int32, (8, 128), 1)
    place = row * 128 + lane
    for h in range(COLS):
        tile = jnp.where(place == 2 * me, ids_ref[2 * h], 0)
        tile = jnp.where(place == 2 * me + 1, ids_ref[2 * h + 1], tile)
        tile = tile.astype(F32).astype(BF16)
        for r in range(ROWS):
            out_ref[r, h, DATA:MESSAGE, :] = tile


def contributions(dest, cluster, velocity, coupling):
    return pl.pallas_call(
        contribution_kernel,
        out_shape=jax.ShapeDtypeStruct((ROWS, COLS, MESSAGE, 128), BF16),
        in_specs=[pl.BlockSpec(memory_space=pltpu.SMEM)] * 2 + [pl.BlockSpec(memory_space=pltpu.HBM)] * 2,
        out_specs=pl.BlockSpec(memory_space=pltpu.VMEM),
        scratch_shapes=[
            pltpu.SMEM((COLS,), jnp.int32),
            pltpu.SMEM((2 * COLS,), jnp.int32),
            pltpu.VMEM((SHELL_DEV, 128, WIDTH), BF16),
            pltpu.VMEM((SHELL_DEV, TOP, 2, PANELS, 128), BF16),
            pltpu.SemaphoreType.DMA((SHELL_DEV + 1,)),
        ],
        compiler_params=pltpu.CompilerParams(vmem_limit_bytes=FIRST_LIMIT),
        name="contributions",
    )(dest.T, cluster.T, velocity, coupling)


def cluster_kernel(got_ref, block_hbm, out_ref, block_ref, total_ref, ids_vec_ref, ids_ref, sem, block_sem):
    block_copy = pltpu.make_async_copy(block_hbm, block_ref, block_sem)
    block_copy.start()
    devices = got_ref.shape[0]
    ids = jnp.zeros((8, 128), F32)
    for s in range(devices):
        ids = ids + got_ref[s, DATA:MESSAGE, :].astype(F32)
    ids_vec_ref[...] = ids.astype(jnp.int32)
    copy = pltpu.make_async_copy(ids_vec_ref, ids_ref, sem)
    copy.start()
    total_ref[...] = jnp.zeros_like(total_ref)
    copy.wait()

    def add(s, carry):
        for slot in range(SLOTS):
            k = ids_ref[s // 64, 2 * (s % 64) + slot]
            piece = got_ref[s, slot * 2 * PIECE : (slot + 1) * 2 * PIECE, :]
            total_ref[k] = total_ref[k] + piece.astype(F32)
        return carry

    lax.fori_loop(0, devices, add, 0, unroll=8)
    out_ref[...] = total_ref[:CLUSTERS].astype(BF16)
    block_copy.wait()


def cluster_sums(got, blocks):
    return pl.pallas_call(
        cluster_kernel,
        out_shape=[
            jax.ShapeDtypeStruct((CLUSTERS, 2 * PIECE, 128), BF16),
            jax.ShapeDtypeStruct(blocks.shape, BF16),
        ],
        in_specs=[pl.BlockSpec(memory_space=pltpu.VMEM), pl.BlockSpec(memory_space=pltpu.HBM)],
        out_specs=[pl.BlockSpec(memory_space=pltpu.VMEM)] * 2,
        scratch_shapes=[
            pltpu.VMEM((CLUSTERS + 1, 2 * PIECE, 128), F32),
            pltpu.VMEM((8, 128), jnp.int32),
            pltpu.SMEM((8, 128), jnp.int32),
            pltpu.SemaphoreType.DMA,
            pltpu.SemaphoreType.DMA,
        ],
        compiler_params=pltpu.CompilerParams(vmem_limit_bytes=VMEM_LIMIT),
        name="cluster_sums",
    )(got, blocks)


def shift_rows(values, pairs):
    return lax.ppermute(values, "row", pairs)


def gather_pieces(own):
    along = [(s, (s + 2) % ROWS if s % 2 == 0 else (s - 2) % ROWS) for s in range(ROWS)]
    twin = [(s, s ^ 1) for s in range(ROWS)]
    near_same = shift_rows(own, along)
    other = shift_rows(own, twin)
    near_other = shift_rows(other, along)
    far_same = shift_rows(near_same, along)
    back_other = shift_rows(near_same, twin)
    back_same = shift_rows(near_other, twin)
    far_other = shift_rows(far_same, twin)
    return [own, near_same, far_same, back_same, other, near_other, far_other, back_other]


def operator_kernel(pairs_ref, *refs):
    piece_refs = refs[:ROWS]
    near_ref, right_ref, left_ref, out_ref, total_ref = refs[ROWS:]
    turn = jnp.where(lax.axis_index("row") % 2 == 0, -1.0, 1.0).astype(F32)

    def rotated(values):
        half = values.shape[0] // 2
        return jnp.concatenate([values[half:], -values[:half]], axis=0) * turn.astype(values.dtype)

    def sources(place):
        code = pairs_ref[place]
        column = code % CLUSTERS
        parts = [
            jnp.concatenate([ref[column, :PIECE], ref[column, PIECE:]], axis=1) for ref in piece_refs
        ]
        return code // CLUSTERS, jnp.concatenate(parts, axis=0)

    total_ref[...] = jnp.zeros_like(total_ref)

    def go(step, carry):
        for j in range(NEAR_STEP):
            owner, values = sources(step * NEAR_STEP + j)
            wide = jnp.concatenate([values, rotated(values)], axis=1)
            i = step * NEAR_STEP + j
            blocks = jnp.concatenate([near_ref[i, 0], near_ref[i, 1]], axis=1)
            total_ref[owner] = total_ref[owner] + dot_t(wide, blocks)
        owners, coeffs = [], []
        for j in range(FAR_STEP):
            owner, values = sources(NEAR + step * FAR_STEP + j)
            owners.append(owner)
            coeffs.append(dot_t(values, right_ref[step * FAR_STEP + j].reshape(2 * RANK, PANELS)))
        for j in range(FAR_STEP):
            value = (coeffs[j][:, :RANK] + rotated(coeffs[j][:, RANK:])).astype(BF16).astype(F32)
            coeffs[j] = jnp.concatenate([value, rotated(value)], axis=1).astype(BF16)
        for j in range(FAR_STEP):
            term = dot_n(coeffs[j], left_ref[step * FAR_STEP + j].reshape(2 * RANK, PANELS))
            total_ref[owners[j]] = total_ref[owners[j]] + term
        return carry

    lax.fori_loop(0, STEPS, go, 0)
    out_ref[...] = total_ref[...].astype(BF16)


def apply_operator(pairs, pieces, near, right, left):
    whole = pl.BlockSpec(memory_space=pltpu.VMEM)
    return pl.pallas_call(
        operator_kernel,
        out_shape=jax.ShapeDtypeStruct((COLS, WIDTH, PANELS), BF16),
        in_specs=[pl.BlockSpec(memory_space=pltpu.SMEM)] + [whole] * (len(pieces) + 3),
        out_specs=whole,
        scratch_shapes=[pltpu.VMEM((COLS, WIDTH, PANELS), F32)],
        compiler_params=pltpu.CompilerParams(vmem_limit_bytes=VMEM_LIMIT),
        name="operator",
    )(pairs, *pieces, near, right, left)


def response_kernel(got_ref, out_ref, rows_ref):
    total = got_ref[0].astype(F32)
    for i in range(1, COLS):
        total = total + got_ref[i].astype(F32)
    me = lax.axis_index("row")
    y, core = me // 2, me % 2
    ahead = jnp.where(core == 0, 3, 1)
    for part in range(2):
        base = jnp.where(part == 0, core, 1 - core) * LOADS
        for i, offset in enumerate((0, ahead, 2, 4 - ahead)):
            start = pl.multiple_of(base + ((y + offset) % 4) * PIECE, PIECE)
            first = part * LOADS + i * PIECE
            rows_ref[pl.ds(start, PIECE), :] = total[first : first + PIECE]
    out_ref[...] = rows_ref[...].T.astype(BF16)


def response_sum(got):
    return pl.pallas_call(
        response_kernel,
        out_shape=jax.ShapeDtypeStruct((PANELS, WIDTH), BF16),
        in_specs=[pl.BlockSpec(memory_space=pltpu.VMEM)],
        out_specs=pl.BlockSpec(memory_space=pltpu.VMEM),
        scratch_shapes=[pltpu.VMEM((WIDTH, PANELS), F32)],
        compiler_params=pltpu.CompilerParams(vmem_limit_bytes=VMEM_LIMIT),
        name="response_sum",
    )(got)


def per_device(velocity, coupling, dest, cluster, near, far_v, far_u, pairs):
    messages = contributions(dest, cluster, velocity, coupling)
    messages = messages.reshape(ROWS * COLS, MESSAGE, 128)
    got = lax.all_to_all(messages, ("row", "col"), split_axis=0, concat_axis=0, tiled=True)
    own, left = cluster_sums(got, far_u[0, 0])
    pieces = gather_pieces(own)
    partial = apply_operator(pairs.reshape(-1), pieces, near[0, 0], far_v[0, 0], left)
    gathered = lax.all_to_all(partial, "col", split_axis=0, concat_axis=0, tiled=True)
    return response_sum(gathered)


def solution(mesh):
    return jax.shard_map(
        per_device,
        mesh=mesh,
        in_specs=(
            P(("row", "col"), None, None),
            P(("row", "col"), None, None, None, None),
            P(("row", "col"), None),
            P(("row", "col"), None),
            P("row", "col", None, None, None, None),
            P("row", "col", None, None, None, None),
            P("row", "col", None, None, None, None),
            P("row", "col", None),
        ),
        out_specs=P(("row", "col"), None),
        check_vma=False,
    )
```

time: 113 us -> 104 us (0.920)
  local copies, waits for them, and re-layouts: 4.09 us -> 0.02 us
  starting transfers between devices: 5.4 us -> 1.69 us
  Pallas kernels: 18.4 us -> 15.9 us
  waiting for transfers between devices: 19.7 us -> 22 us
    unnamed x12 -> x8, local copies, waits for them, and re-layouts: 4.06 us -> 0.02 us
    ppermute x9 -> x7, starting transfers between devices: 5.4 us -> 1.69 us  [shift_rows(): return lax.ppermute(values, 'row', pairs)]
    pallas_call x3, Pallas kernels: 17.5 us -> 15 us  [the longest x1 6.88 us: apply_operator(): pl.pallas_call(operator_kernel, out_shape=jax.ShapeDtypeStruct((COLS, WID...]
    ppermute x9 -> x7, waiting for transfers between devices: 19.7 us -> 22 us  [shift_rows(): return lax.ppermute(values, 'row', pairs)]
  transfers between devices with their start and end apart: 9 -> 7, of which waited for: 4 -> 5; matrix products, arithmetic and copies ran while one was open for 0% -> 0% of each run, Pallas kernels for 0% -> 0%
where the time goes in v2:
time: 104 us
  blocking collectives  64.5 us (62%)
  waiting for transfers between devices  22 us (21%)
  Pallas kernels  15.9 us (15%)
  starting transfers between devices  1.69 us (2%)
    all_to_all x1, blocking collectives, per_device(): lax.all_to_all(messages, ('row', 'col'), split_axis=0, concat_axis=0, til...  43.5 us
    ppermute x7, waiting for transfers between devices, shift_rows(): return lax.ppermute(values, 'row', pairs)  22 us
    all_to_all x1, blocking collectives, per_device(): lax.all_to_all(partial, 'col', split_axis=0, concat_axis=0, tiled=True)  21 us
    pallas_call x1, Pallas kernels, apply_operator(): pl.pallas_call(operator_kernel, out_shape=jax.ShapeDtypeStruct((COLS, WID...  6.88 us
    pallas_call x1, Pallas kernels, contributions(): pl.pallas_call(contribution_kernel, out_shape=jax.ShapeDtypeStruct((ROWS,...  5.7 us
    pallas_call x1, Pallas kernels, cluster_sums(): pl.pallas_call(cluster_kernel, out_shape=[jax.ShapeDtypeStruct((CLUSTERS,...  2.47 us
  transfers between devices with their start and end apart: 7, of which 5 were waited for; matrix products, arithmetic and copies ran while one was open for 0% of the time, Pallas kernels for 0%

profile of v2, /device:TPU:0, one launch (start us, length us, event | category | flops | bytes accessed | tf_op | source)
XLA Modules:
  0.0 104.2 jit_solution(13162149099303005972)
XLA Ops:
  0.0 0.0 copy-start.2
  0.0 0.0 copy-start.1
  0.0 5.7 %contributions.1 = bf16[8,16,72,128]{3,2,1,0:T(8,128)(2,1)} custom-call(s32[2,8]{1,0:T(2,128)} %bitcast.12, s32[2,8]{1,0:T(2,128)} %bitcast.13, bf16[8,128,128]{2,1,0:T(8,128)(2,1)} %velocity_hbm.1, bf16[8,2,2,256,128]{4,3,2,1,0:T(8,128)(2,1)} %coupling_hbm.1), custom_call_target="tpu_custom_call" | custom-call | tf_op jit(solution)/shard_map/contributions/pallas_call | solution.py:92
  5.7 0.0 copy-start
  5.7 43.5 %all_to_all.10.got_ref = bf16[128,72,128]{2,1,0:T(8,128)(2,1)S(1)} all-to-all(bf16[128,72,128]{2,1,0:T(8,128)(2,1)} %bitcast.11), channel_id=1, replica_groups=mesh['row'=8,'col'=16] {'row','col'}, dimensions={0} | all-to-all | bytes 4718592 | tf_op jit(solution)/shard_map/all_to_all | solution.py:259
  49.2 0.0 copy-done.2
  49.2 0.0 copy-start.3
  49.2 2.5 %cluster_sums.1 = (bf16[64,32,128]{2,1,0:T(8,128)(2,1)S(1)}, bf16[64,2,32,256]{3,2,1,0:T(8,128)(2,1)S(1)}) custom-call(bf16[128,72,128]{2,1,0:T(8,128)(2,1)S(1)} %all_to_all.10.got_ref, bf16[64,2,32,256]{3,2,1,0:T(8,128)(2,1)S(1)} %bitcast.9), custom_call_target="tpu_custom_call" | custom-call | tf_op jit(solution)/shard_map/cluster_sums/pallas_call | solution.py:135
  51.7 0.1 collective-permute-start.2
  51.8 0.7 collective-permute-start
  52.5 1.2 %collective-permute-done.2.refs_4_ = bf16[64,32,128]{2,1,0:T(8,128)(2,1)S(1)} collective-permute-done((bf16[64,32,128]{2,1,0:T(8,128)(2,1)S(1)}, bf16[64,32,128]{2,1,0:T(8,128)(2,1)S(1)}, u32[]{:S(2)}, u32[]{:S(2)}) %collective-permute-start.2) | collective-permute-done | bytes 524320 | tf_op jit(solution)/shard_map/ppermute | solution.py:156
  53.7 0.6 collective-permute-start.3
  54.3 7.9 %collective-permute-done.refs_1_ = bf16[64,32,128]{2,1,0:T(8,128)(2,1)S(1)} collective-permute-done((bf16[64,32,128]{2,1,0:T(8,128)(2,1)S(1)}, bf16[64,32,128]{2,1,0:T(8,128)(2,1)S(1)}, u32[]{:S(2)}, u32[]{:S(2)}) %collective-permute-start) | collective-permute-done | bytes 524320 | tf_op jit(solution)/shard_map/ppermute | solution.py:156
  62.3 0.0 collective-permute-start.1
  62.3 0.3 collective-permute-start.6
  62.5 5.3 %collective-permute-done.3.refs_5_ = bf16[64,32,128]{2,1,0:T(8,128)(2,1)S(1)} collective-permute-done((bf16[64,32,128]{2,1,0:T(8,128)(2,1)S(1)}, bf16[64,32,128]{2,1,0:T(8,128)(2,1)S(1)}, u32[]{:S(2)}, u32[]{:S(2)}) %collective-permute-start.3) | collective-permute-done | bytes 524320 | tf_op jit(solution)/shard_map/ppermute | solution.py:156
  67.9 0.0 collective-permute-start.4
  67.9 5.6 %collective-permute-done.1.refs_2_ = bf16[64,32,128]{2,1,0:T(8,128)(2,1)S(1)} collective-permute-done((bf16[64,32,128]{2,1,0:T(8,128)(2,1)S(1)}, bf16[64,32,128]{2,1,0:T(8,128)(2,1)S(1)}, u32[]{:S(2)}, u32[]{:S(2)}) %collective-permute-start.1) | collective-permute-done | bytes 524320 | tf_op jit(solution)/shard_map/ppermute | solution.py:156
  73.5 0.0 collective-permute-start.5
  73.5 0.0 collective-permute-done.6.refs_7_
  73.5 0.0 collective-permute-done.4.refs_3_
  73.5 1.9 %collective-permute-done.5.refs_6_ = bf16[64,32,128]{2,1,0:T(8,128)(2,1)S(1)} collective-permute-done((bf16[64,32,128]{2,1,0:T(8,128)(2,1)S(1)}, bf16[64,32,128]{2,1,0:T(8,128)(2,1)S(1)}, u32[]{:S(2)}, u32[]{:S(2)}) %collective-permute-start.5) | collective-permute-done | bytes 524320 | tf_op jit(solution)/shard_map/ppermute | solution.py:156
  75.4 0.0 copy-done.1
  75.4 0.0 copy-done
  75.4 0.0 copy-done.3
  75.4 6.9 %operator.1 = bf16[16,128,256]{2,1,0:T(8,128)(2,1)S(1)} custom-call(s32[96]{0:T(128)S(1)} %bitcast.10, bf16[64,32,128]{2,1,0:T(8,128)(2,1)S(1)} %get-tuple-element.7.refs_0_, bf16[64,32,128]{2,1,0:T(8,128)(2,1)S(1)} %collective-permute-done.refs_1_, bf16[64,32,128]{2,1,0:T(8,128)(2,1)S(1)} %collective-permute-done.1.refs_2_, ...), custom_call_target="tpu_custom_call" | custom-call | tf_op jit(solution)/shard_map/operator/pallas_call | solution.py:217
  82.3 21.0 %all_to_all.11.got_ref = bf16[16,128,256]{2,1,0:T(8,128)(2,1)S(1)} all-to-all(bf16[16,128,256]{2,1,0:T(8,128)(2,1)S(1)} %operator.1), channel_id=1, replica_groups=mesh['row'=8,'col'=16] {'col'}, dimensions={0} | all-to-all | bytes 2097152 | tf_op jit(solution)/shard_map/all_to_all | solution.py:263
  103.3 0.9 response_sum.1
Async XLA Ops:
  0.0 49.2 %copy-start.2 = (bf16[1,1,64,2,32,256]{5,4,3,2,1,0:T(8,128)(2,1)S(1)}, bf16[1,1,64,2,32,256]{5,4,3,2,1,0:T(8,128)(2,1)}, u32[]{:S(2)}) copy-start(bf16[1,1,64,2,32,256]{5,4,3,2,1,0:T(8,128)(2,1)} %param.14) | copy-start | bytes 6291460
  0.0 75.4 %copy-start.1 = (bf16[1,1,64,2,32,256]{5,4,3,2,1,0:T(8,128)(2,1)S(1)}, bf16[1,1,64,2,32,256]{5,4,3,2,1,0:T(8,128)(2,1)}, u32[]{:S(2)}) copy-start(bf16[1,1,64,2,32,256]{5,4,3,2,1,0:T(8,128)(2,1)} %param.13) | copy-start | bytes 6291460
  5.7 69.7 %copy-start = (bf16[1,1,32,2,256,256]{5,4,3,2,1,0:T(8,128)(2,1)S(1)}, bf16[1,1,32,2,256,256]{5,4,3,2,1,0:T(8,128)(2,1)}, u32[]{:S(2)}) copy-start(bf16[1,1,32,2,256,256]{5,4,3,2,1,0:T(8,128)(2,1)} %param.12) | copy-start | bytes 25165828
  49.2 26.2 %copy-start.3 = (s32[1,1,96]{2,1,0:T(1,128)S(1)}, s32[1,1,96]{2,1,0:T(1,128)}, u32[]{:S(2)}) copy-start(s32[1,1,96]{2,1,0:T(1,128)} %param.15) | copy-start | bytes 1156
  51.7 2.0 %collective-permute-start.2 = (bf16[64,32,128]{2,1,0:T(8,128)(2,1)S(1)}, bf16[64,32,128]{2,1,0:T(8,128)(2,1)S(1)}, u32[]{:S(2)}, u32[]{:S(2)}) collective-permute-start(bf16[64,32,128]{2,1,0:T(8,128)(2,1)S(1)} %get-tuple-element.7.refs_0_), channel_id=1, source_target_pairs={{0,16},{16,0},{32,48},{48,32},{64,80},{80,64},{96,112},{112,96},{1... | collective-permute-start | bytes 1572872 | tf_op jit(solution)/shard_map/ppermute | solution.py:156
  51.8 10.5 %collective-permute-start = (bf16[64,32,128]{2,1,0:T(8,128)(2,1)S(1)}, bf16[64,32,128]{2,1,0:T(8,128)(2,1)S(1)}, u32[]{:S(2)}, u32[]{:S(2)}) collective-permute-start(bf16[64,32,128]{2,1,0:T(8,128)(2,1)S(1)} %get-tuple-element.7.refs_0_), channel_id=1, source_target_pairs={{0,32},{16,112},{32,64},{48,16},{64,96},{80,48},{96,0},{112,80},{1... | collective-permute-start | bytes 1572872 | tf_op jit(solution)/shard_map/ppermute | solution.py:156
  53.7 14.2 %collective-permute-start.3 = (bf16[64,32,128]{2,1,0:T(8,128)(2,1)S(1)}, bf16[64,32,128]{2,1,0:T(8,128)(2,1)S(1)}, u32[]{:S(2)}, u32[]{:S(2)}) collective-permute-start(bf16[64,32,128]{2,1,0:T(8,128)(2,1)S(1)} %collective-permute-done.2.refs_4_), channel_id=1, source_target_pairs={{0,32},{16,112},{32,64},{48,16},{64,96},{80,48},{96,0},{112,80},{1... | collective-permute-start | bytes 1572872 | tf_op jit(solution)/shard_map/ppermute | solution.py:156
  62.3 11.2 %collective-permute-start.1 = (bf16[64,32,128]{2,1,0:T(8,128)(2,1)S(1)}, bf16[64,32,128]{2,1,0:T(8,128)(2,1)S(1)}, u32[]{:S(2)}, u32[]{:S(2)}) collective-permute-start(bf16[64,32,128]{2,1,0:T(8,128)(2,1)S(1)} %collective-permute-done.refs_1_), channel_id=1, source_target_pairs={{0,32},{16,112},{32,64},{48,16},{64,96},{80,48},{96,0},{112,80},{1... | collective-permute-start | bytes 1572872 | tf_op jit(solution)/shard_map/ppermute | solution.py:156
  62.3 11.2 %collective-permute-start.6 = (bf16[64,32,128]{2,1,0:T(8,128)(2,1)S(1)}, bf16[64,32,128]{2,1,0:T(8,128)(2,1)S(1)}, u32[]{:S(2)}, u32[]{:S(2)}) collective-permute-start(bf16[64,32,128]{2,1,0:T(8,128)(2,1)S(1)} %collective-permute-done.refs_1_), channel_id=1, source_target_pairs={{0,16},{16,0},{32,48},{48,32},{64,80},{80,64},{96,112},{112,96},{1... | collective-permute-start | bytes 1572872 | tf_op jit(solution)/shard_map/ppermute | solution.py:156
  67.9 5.6 %collective-permute-start.4 = (bf16[64,32,128]{2,1,0:T(8,128)(2,1)S(1)}, bf16[64,32,128]{2,1,0:T(8,128)(2,1)S(1)}, u32[]{:S(2)}, u32[]{:S(2)}) collective-permute-start(bf16[64,32,128]{2,1,0:T(8,128)(2,1)S(1)} %collective-permute-done.3.refs_5_), channel_id=1, source_target_pairs={{0,16},{16,0},{32,48},{48,32},{64,80},{80,64},{96,112},{112,96},{1... | collective-permute-start | bytes 1572872 | tf_op jit(solution)/shard_map/ppermute | solution.py:156
  73.5 1.9 %collective-permute-start.5 = (bf16[64,32,128]{2,1,0:T(8,128)(2,1)S(1)}, bf16[64,32,128]{2,1,0:T(8,128)(2,1)S(1)}, u32[]{:S(2)}, u32[]{:S(2)}) collective-permute-start(bf16[64,32,128]{2,1,0:T(8,128)(2,1)S(1)} %collective-permute-done.1.refs_2_), channel_id=1, source_target_pairs={{0,16},{16,0},{32,48},{48,32},{64,80},{80,64},{96,112},{112,96},{1... | collective-permute-start | bytes 1572872 | tf_op jit(solution)/shard_map/ppermute | solution.py:156

commit v3 on v2

--- a/solution.py
+++ b/solution.py
@@ -19,8 +19,8 @@
 PIECE = WIDTH // ROWS
 DATA = SLOTS * 2 * PIECE
 MESSAGE = DATA + 8
-NEAR_STEP = 8
-FAR_STEP = 16
+NEAR_STEP = 16
+FAR_STEP = 32
 RANK = 32
 STEPS = NEAR // NEAR_STEP
 VMEM_LIMIT = 12 * 1024 * 1024
@@ -44,14 +44,30 @@
 
 
 def contribution_kernel(
-    dest_ref, cluster_ref, velocity_hbm, coupling_hbm, out_ref, count_ref, ids_ref, velocity_ref, coupling_ref, sem
+    dest_hbm,
+    cluster_hbm,
+    velocity_hbm,
+    coupling_hbm,
+    out_ref,
+    dest_ref,
+    cluster_ref,
+    count_ref,
+    ids_ref,
+    velocity_ref,
+    coupling_ref,
+    sem,
 ):
+    dest_copy = pltpu.make_async_copy(dest_hbm, dest_ref, sem.at[SHELL_DEV + 1])
+    cluster_copy = pltpu.make_async_copy(cluster_hbm, cluster_ref, sem.at[SHELL_DEV + 2])
     velocity_copy = pltpu.make_async_copy(velocity_hbm, velocity_ref, sem.at[SHELL_DEV])
     copies = [
         pltpu.make_async_copy(coupling_hbm.at[s], coupling_ref.at[s], sem.at[s]) for s in range(SHELL_DEV)
     ]
     velocity_copy.start()
-    for copy in copies:
+    copies[0].start()
+    dest_copy.start()
+    cluster_copy.start()
+    for copy in copies[1:]:
         copy.start()
     for h in range(COLS):
         count_ref[h] = 0
@@ -62,6 +78,9 @@
         velocity = velocity_ref[s].astype(F32).T
         wide = jnp.concatenate([velocity, rotate_rows(velocity)], axis=1).astype(BF16)
         copies[s].wait()
+        if s == 0:
+            dest_copy.wait()
+            cluster_copy.wait()
         for t in range(TOP):
             h = dest_ref[t, s]
             slot = jnp.minimum(count_ref[h], SLOTS - 1)
@@ -92,14 +111,16 @@
     return pl.pallas_call(
         contribution_kernel,
         out_shape=jax.ShapeDtypeStruct((ROWS, COLS, MESSAGE, 128), BF16),
-        in_specs=[pl.BlockSpec(memory_space=pltpu.SMEM)] * 2 + [pl.BlockSpec(memory_space=pltpu.HBM)] * 2,
+        in_specs=[pl.BlockSpec(memory_space=pltpu.HBM)] * 4,
         out_specs=pl.BlockSpec(memory_space=pltpu.VMEM),
         scratch_shapes=[
+            pltpu.SMEM((TOP, SHELL_DEV), jnp.int32),
+            pltpu.SMEM((TOP, SHELL_DEV), jnp.int32),
             pltpu.SMEM((COLS,), jnp.int32),
             pltpu.SMEM((2 * COLS,), jnp.int32),
             pltpu.VMEM((SHELL_DEV, 128, WIDTH), BF16),
             pltpu.VMEM((SHELL_DEV, TOP, 2, PANELS, 128), BF16),
-            pltpu.SemaphoreType.DMA((SHELL_DEV + 1,)),
+            pltpu.SemaphoreType.DMA((SHELL_DEV + 3,)),
         ],
         compiler_params=pltpu.CompilerParams(vmem_limit_bytes=FIRST_LIMIT),
         name="contributions",

time: 104 us -> 103 us (level)
  Pallas kernels: 15.9 us -> 14.4 us
    pallas_call x1, Pallas kernels: 5.7 us -> 4.63 us  [contributions(): pl.pallas_call(contribution_kernel, out_shape=jax.ShapeDtypeStruct((ROWS,...]
where the time goes in v3:
time: 103 us
  blocking collectives  64.5 us (63%)
  waiting for transfers between devices  22 us (21%)
  Pallas kernels  14.4 us (14%)
  starting transfers between devices  1.69 us (2%)
    all_to_all x1, blocking collectives, per_device(): lax.all_to_all(messages, ('row', 'col'), split_axis=0, concat_axis=0, til...  43.5 us
    ppermute x7, waiting for transfers between devices, shift_rows(): return lax.ppermute(values, 'row', pairs)  22 us
    all_to_all x1, blocking collectives, per_device(): lax.all_to_all(partial, 'col', split_axis=0, concat_axis=0, tiled=True)  21 us
    pallas_call x1, Pallas kernels, apply_operator(): pl.pallas_call(operator_kernel, out_shape=jax.ShapeDtypeStruct((COLS, WID...  6.46 us
    pallas_call x1, Pallas kernels, contributions(): pl.pallas_call(contribution_kernel, out_shape=jax.ShapeDtypeStruct((ROWS,...  4.63 us
    pallas_call x1, Pallas kernels, cluster_sums(): pl.pallas_call(cluster_kernel, out_shape=[jax.ShapeDtypeStruct((CLUSTERS,...  2.46 us
  transfers between devices with their start and end apart: 7, of which 5 were waited for; matrix products, arithmetic and copies ran while one was open for 0% of the time, Pallas kernels for 0%

profile of v3, /device:TPU:0, one launch (start us, length us, event | category | flops | bytes accessed | tf_op | source)
XLA Modules:
  0.0 102.7 jit_solution(6345870454891714458)
XLA Ops:
  0.0 0.0 copy-start.2
  0.0 0.0 copy-start.1
  0.0 4.6 %contributions.1 = bf16[8,16,72,128]{3,2,1,0:T(8,128)(2,1)} custom-call(s32[2,8]{1,0:T(2,128)} %bitcast.12, s32[2,8]{1,0:T(2,128)} %bitcast.13, bf16[8,128,128]{2,1,0:T(8,128)(2,1)} %velocity_hbm.1, bf16[8,2,2,256,128]{4,3,2,1,0:T(8,128)(2,1)} %coupling_hbm.1), custom_call_target="tpu_custom_call" | custom-call | tf_op jit(solution)/shard_map/contributions/pallas_call | solution.py:111
  4.6 0.0 copy-start
  4.7 43.5 %all_to_all.10.got_ref = bf16[128,72,128]{2,1,0:T(8,128)(2,1)S(1)} all-to-all(bf16[128,72,128]{2,1,0:T(8,128)(2,1)} %bitcast.11), channel_id=1, replica_groups=mesh['row'=8,'col'=16] {'row','col'}, dimensions={0} | all-to-all | bytes 4718592 | tf_op jit(solution)/shard_map/all_to_all | solution.py:280
  48.2 0.0 copy-done.2
  48.2 0.0 copy-start.3
  48.2 2.5 %cluster_sums.1 = (bf16[64,32,128]{2,1,0:T(8,128)(2,1)S(1)}, bf16[64,2,32,256]{3,2,1,0:T(8,128)(2,1)S(1)}) custom-call(bf16[128,72,128]{2,1,0:T(8,128)(2,1)S(1)} %all_to_all.10.got_ref, bf16[64,2,32,256]{3,2,1,0:T(8,128)(2,1)S(1)} %bitcast.9), custom_call_target="tpu_custom_call" | custom-call | tf_op jit(solution)/shard_map/cluster_sums/pallas_call | solution.py:156
  50.6 0.1 collective-permute-start.2
  50.7 0.7 collective-permute-start
  51.4 1.2 %collective-permute-done.2.refs_4_ = bf16[64,32,128]{2,1,0:T(8,128)(2,1)S(1)} collective-permute-done((bf16[64,32,128]{2,1,0:T(8,128)(2,1)S(1)}, bf16[64,32,128]{2,1,0:T(8,128)(2,1)S(1)}, u32[]{:S(2)}, u32[]{:S(2)}) %collective-permute-start.2) | collective-permute-done | bytes 524320 | tf_op jit(solution)/shard_map/ppermute | solution.py:177
  52.6 0.6 collective-permute-start.3
  53.3 7.9 %collective-permute-done.refs_1_ = bf16[64,32,128]{2,1,0:T(8,128)(2,1)S(1)} collective-permute-done((bf16[64,32,128]{2,1,0:T(8,128)(2,1)S(1)}, bf16[64,32,128]{2,1,0:T(8,128)(2,1)S(1)}, u32[]{:S(2)}, u32[]{:S(2)}) %collective-permute-start) | collective-permute-done | bytes 524320 | tf_op jit(solution)/shard_map/ppermute | solution.py:177
  61.2 0.0 collective-permute-start.1
  61.2 0.3 collective-permute-start.6
  61.5 5.3 %collective-permute-done.3.refs_5_ = bf16[64,32,128]{2,1,0:T(8,128)(2,1)S(1)} collective-permute-done((bf16[64,32,128]{2,1,0:T(8,128)(2,1)S(1)}, bf16[64,32,128]{2,1,0:T(8,128)(2,1)S(1)}, u32[]{:S(2)}, u32[]{:S(2)}) %collective-permute-start.3) | collective-permute-done | bytes 524320 | tf_op jit(solution)/shard_map/ppermute | solution.py:177
  66.8 0.0 collective-permute-start.4
  66.8 5.6 %collective-permute-done.1.refs_2_ = bf16[64,32,128]{2,1,0:T(8,128)(2,1)S(1)} collective-permute-done((bf16[64,32,128]{2,1,0:T(8,128)(2,1)S(1)}, bf16[64,32,128]{2,1,0:T(8,128)(2,1)S(1)}, u32[]{:S(2)}, u32[]{:S(2)}) %collective-permute-start.1) | collective-permute-done | bytes 524320 | tf_op jit(solution)/shard_map/ppermute | solution.py:177
  72.4 0.0 collective-permute-start.5
  72.4 0.0 collective-permute-done.6.refs_7_
  72.4 0.0 collective-permute-done.4.refs_3_
  72.4 1.9 %collective-permute-done.5.refs_6_ = bf16[64,32,128]{2,1,0:T(8,128)(2,1)S(1)} collective-permute-done((bf16[64,32,128]{2,1,0:T(8,128)(2,1)S(1)}, bf16[64,32,128]{2,1,0:T(8,128)(2,1)S(1)}, u32[]{:S(2)}, u32[]{:S(2)}) %collective-permute-start.5) | collective-permute-done | bytes 524320 | tf_op jit(solution)/shard_map/ppermute | solution.py:177
  74.3 0.0 copy-done.1
  74.3 0.0 copy-done
  74.3 0.0 copy-done.3
  74.3 6.5 %operator.1 = bf16[16,128,256]{2,1,0:T(8,128)(2,1)S(1)} custom-call(s32[96]{0:T(128)S(1)} %bitcast.10, bf16[64,32,128]{2,1,0:T(8,128)(2,1)S(1)} %get-tuple-element.7.refs_0_, bf16[64,32,128]{2,1,0:T(8,128)(2,1)S(1)} %collective-permute-done.refs_1_, bf16[64,32,128]{2,1,0:T(8,128)(2,1)S(1)} %collective-permute-done.1.refs_2_, ...), custom_call_target="tpu_custom_call" | custom-call | tf_op jit(solution)/shard_map/operator/pallas_call | solution.py:238
  80.8 21.0 %all_to_all.11.got_ref = bf16[16,128,256]{2,1,0:T(8,128)(2,1)S(1)} all-to-all(bf16[16,128,256]{2,1,0:T(8,128)(2,1)S(1)} %operator.1), channel_id=1, replica_groups=mesh['row'=8,'col'=16] {'col'}, dimensions={0} | all-to-all | bytes 2097152 | tf_op jit(solution)/shard_map/all_to_all | solution.py:284
  101.8 0.9 response_sum.1
Async XLA Ops:
  0.0 48.2 %copy-start.2 = (bf16[1,1,64,2,32,256]{5,4,3,2,1,0:T(8,128)(2,1)S(1)}, bf16[1,1,64,2,32,256]{5,4,3,2,1,0:T(8,128)(2,1)}, u32[]{:S(2)}) copy-start(bf16[1,1,64,2,32,256]{5,4,3,2,1,0:T(8,128)(2,1)} %param.14) | copy-start | bytes 6291460
  0.0 74.3 %copy-start.1 = (bf16[1,1,64,2,32,256]{5,4,3,2,1,0:T(8,128)(2,1)S(1)}, bf16[1,1,64,2,32,256]{5,4,3,2,1,0:T(8,128)(2,1)}, u32[]{:S(2)}) copy-start(bf16[1,1,64,2,32,256]{5,4,3,2,1,0:T(8,128)(2,1)} %param.13) | copy-start | bytes 6291460
  4.6 69.7 %copy-start = (bf16[1,1,32,2,256,256]{5,4,3,2,1,0:T(8,128)(2,1)S(1)}, bf16[1,1,32,2,256,256]{5,4,3,2,1,0:T(8,128)(2,1)}, u32[]{:S(2)}) copy-start(bf16[1,1,32,2,256,256]{5,4,3,2,1,0:T(8,128)(2,1)} %param.12) | copy-start | bytes 25165828
  48.2 26.2 %copy-start.3 = (s32[1,1,96]{2,1,0:T(1,128)S(1)}, s32[1,1,96]{2,1,0:T(1,128)}, u32[]{:S(2)}) copy-start(s32[1,1,96]{2,1,0:T(1,128)} %param.15) | copy-start | bytes 1156
  50.6 2.0 %collective-permute-start.2 = (bf16[64,32,128]{2,1,0:T(8,128)(2,1)S(1)}, bf16[64,32,128]{2,1,0:T(8,128)(2,1)S(1)}, u32[]{:S(2)}, u32[]{:S(2)}) collective-permute-start(bf16[64,32,128]{2,1,0:T(8,128)(2,1)S(1)} %get-tuple-element.7.refs_0_), channel_id=1, source_target_pairs={{0,16},{16,0},{32,48},{48,32},{64,80},{80,64},{96,112},{112,96},{1... | collective-permute-start | bytes 1572872 | tf_op jit(solution)/shard_map/ppermute | solution.py:177
  50.7 10.5 %collective-permute-start = (bf16[64,32,128]{2,1,0:T(8,128)(2,1)S(1)}, bf16[64,32,128]{2,1,0:T(8,128)(2,1)S(1)}, u32[]{:S(2)}, u32[]{:S(2)}) collective-permute-start(bf16[64,32,128]{2,1,0:T(8,128)(2,1)S(1)} %get-tuple-element.7.refs_0_), channel_id=1, source_target_pairs={{0,32},{16,112},{32,64},{48,16},{64,96},{80,48},{96,0},{112,80},{1... | collective-permute-start | bytes 1572872 | tf_op jit(solution)/shard_map/ppermute | solution.py:177
  52.6 14.2 %collective-permute-start.3 = (bf16[64,32,128]{2,1,0:T(8,128)(2,1)S(1)}, bf16[64,32,128]{2,1,0:T(8,128)(2,1)S(1)}, u32[]{:S(2)}, u32[]{:S(2)}) collective-permute-start(bf16[64,32,128]{2,1,0:T(8,128)(2,1)S(1)} %collective-permute-done.2.refs_4_), channel_id=1, source_target_pairs={{0,32},{16,112},{32,64},{48,16},{64,96},{80,48},{96,0},{112,80},{1... | collective-permute-start | bytes 1572872 | tf_op jit(solution)/shard_map/ppermute | solution.py:177
  61.2 11.2 %collective-permute-start.1 = (bf16[64,32,128]{2,1,0:T(8,128)(2,1)S(1)}, bf16[64,32,128]{2,1,0:T(8,128)(2,1)S(1)}, u32[]{:S(2)}, u32[]{:S(2)}) collective-permute-start(bf16[64,32,128]{2,1,0:T(8,128)(2,1)S(1)} %collective-permute-done.refs_1_), channel_id=1, source_target_pairs={{0,32},{16,112},{32,64},{48,16},{64,96},{80,48},{96,0},{112,80},{1... | collective-permute-start | bytes 1572872 | tf_op jit(solution)/shard_map/ppermute | solution.py:177
  61.2 11.2 %collective-permute-start.6 = (bf16[64,32,128]{2,1,0:T(8,128)(2,1)S(1)}, bf16[64,32,128]{2,1,0:T(8,128)(2,1)S(1)}, u32[]{:S(2)}, u32[]{:S(2)}) collective-permute-start(bf16[64,32,128]{2,1,0:T(8,128)(2,1)S(1)} %collective-permute-done.refs_1_), channel_id=1, source_target_pairs={{0,16},{16,0},{32,48},{48,32},{64,80},{80,64},{96,112},{112,96},{1... | collective-permute-start | bytes 1572872 | tf_op jit(solution)/shard_map/ppermute | solution.py:177
  66.8 5.6 %collective-permute-start.4 = (bf16[64,32,128]{2,1,0:T(8,128)(2,1)S(1)}, bf16[64,32,128]{2,1,0:T(8,128)(2,1)S(1)}, u32[]{:S(2)}, u32[]{:S(2)}) collective-permute-start(bf16[64,32,128]{2,1,0:T(8,128)(2,1)S(1)} %collective-permute-done.3.refs_5_), channel_id=1, source_target_pairs={{0,16},{16,0},{32,48},{48,32},{64,80},{80,64},{96,112},{112,96},{1... | collective-permute-start | bytes 1572872 | tf_op jit(solution)/shard_map/ppermute | solution.py:177
  72.4 1.9 %collective-permute-start.5 = (bf16[64,32,128]{2,1,0:T(8,128)(2,1)S(1)}, bf16[64,32,128]{2,1,0:T(8,128)(2,1)S(1)}, u32[]{:S(2)}, u32[]{:S(2)}) collective-permute-start(bf16[64,32,128]{2,1,0:T(8,128)(2,1)S(1)} %collective-permute-done.1.refs_2_), channel_id=1, source_target_pairs={{0,16},{16,0},{32,48},{48,32},{64,80},{80,64},{96,112},{112,96},{1... | collective-permute-start | bytes 1572872 | tf_op jit(solution)/shard_map/ppermute | solution.py:177

commit v4 on v3

--- a/solution.py
+++ b/solution.py
@@ -75,8 +75,8 @@
         ids_ref[2 * h + 1] = CLUSTERS
     velocity_copy.wait()
     for s in range(SHELL_DEV):
-        velocity = velocity_ref[s].astype(F32).T
-        wide = jnp.concatenate([velocity, rotate_rows(velocity)], axis=1).astype(BF16)
+        velocity = velocity_ref[s].T
+        wide = jnp.concatenate([velocity, rotate_rows(velocity)], axis=1)
         copies[s].wait()
         if s == 0:
             dest_copy.wait()
@@ -127,7 +127,7 @@
     )(dest.T, cluster.T, velocity, coupling)
 
 
-def cluster_kernel(got_ref, block_hbm, out_ref, block_ref, total_ref, ids_vec_ref, ids_ref, sem, block_sem):
+def cluster_kernel(got_ref, block_hbm, out_ref, block_ref, total_ref, other_ref, ids_vec_ref, ids_ref, sem, block_sem):
     block_copy = pltpu.make_async_copy(block_hbm, block_ref, block_sem)
     block_copy.start()
     devices = got_ref.shape[0]
@@ -138,17 +138,20 @@
     copy = pltpu.make_async_copy(ids_vec_ref, ids_ref, sem)
     copy.start()
     total_ref[...] = jnp.zeros_like(total_ref)
+    other_ref[...] = jnp.zeros_like(other_ref)
     copy.wait()
 
-    def add(s, carry):
-        for slot in range(SLOTS):
-            k = ids_ref[s // 64, 2 * (s % 64) + slot]
-            piece = got_ref[s, slot * 2 * PIECE : (slot + 1) * 2 * PIECE, :]
-            total_ref[k] = total_ref[k] + piece.astype(F32)
-        return carry
-
-    lax.fori_loop(0, devices, add, 0, unroll=8)
-    out_ref[...] = total_ref[:CLUSTERS].astype(BF16)
+    for row in range(devices // 64):
+
+        def add(i, carry):
+            for slot, sums_ref in enumerate((total_ref, other_ref)):
+                k = ids_ref[row, 2 * i + slot]
+                piece = got_ref[row * 64 + i, slot * 2 * PIECE : (slot + 1) * 2 * PIECE, :]
+                sums_ref[k] = sums_ref[k] + piece.astype(F32)
+            return carry
+
+        lax.fori_loop(0, 64, add, 0, unroll=8)
+    out_ref[...] = (total_ref[:CLUSTERS] + other_ref[:CLUSTERS]).astype(BF16)
     block_copy.wait()
 
 
@@ -162,6 +165,7 @@
         in_specs=[pl.BlockSpec(memory_space=pltpu.VMEM), pl.BlockSpec(memory_space=pltpu.HBM)],
         out_specs=[pl.BlockSpec(memory_space=pltpu.VMEM)] * 2,
         scratch_shapes=[
+            pltpu.VMEM((CLUSTERS + 1, 2 * PIECE, 128), F32),
             pltpu.VMEM((CLUSTERS + 1, 2 * PIECE, 128), F32),
             pltpu.VMEM((8, 128), jnp.int32),
             pltpu.SMEM((8, 128), jnp.int32),
@@ -222,8 +226,8 @@
             owners.append(owner)
             coeffs.append(dot_t(values, right_ref[step * FAR_STEP + j].reshape(2 * RANK, PANELS)))
         for j in range(FAR_STEP):
-            value = (coeffs[j][:, :RANK] + rotated(coeffs[j][:, RANK:])).astype(BF16).astype(F32)
-            coeffs[j] = jnp.concatenate([value, rotated(value)], axis=1).astype(BF16)
+            value = (coeffs[j][:, :RANK] + rotated(coeffs[j][:, RANK:])).astype(BF16)
+            coeffs[j] = jnp.concatenate([value, rotated(value)], axis=1)
         for j in range(FAR_STEP):
             term = dot_n(coeffs[j], left_ref[step * FAR_STEP + j].reshape(2 * RANK, PANELS))
             total_ref[owners[j]] = total_ref[owners[j]] + term

time: 103 us -> 102 us (level)
  no operation moved by 1% of the time
where the time goes in v4:
time: 102 us
  blocking collectives  64.5 us (63%)
  waiting for transfers between devices  22 us (22%)
  Pallas kernels  13.7 us (13%)
  starting transfers between devices  1.69 us (2%)
    all_to_all x1, blocking collectives, per_device(): lax.all_to_all(messages, ('row', 'col'), split_axis=0, concat_axis=0, til...  43.5 us
    ppermute x7, waiting for transfers between devices, shift_rows(): return lax.ppermute(values, 'row', pairs)  22 us
    all_to_all x1, blocking collectives, per_device(): lax.all_to_all(partial, 'col', split_axis=0, concat_axis=0, tiled=True)  21 us
    pallas_call x1, Pallas kernels, apply_operator(): pl.pallas_call(operator_kernel, out_shape=jax.ShapeDtypeStruct((COLS, WID...  6.24 us
    pallas_call x1, Pallas kernels, contributions(): pl.pallas_call(contribution_kernel, out_shape=jax.ShapeDtypeStruct((ROWS,...  4.61 us
  transfers between devices with their start and end apart: 7, of which 5 were waited for; matrix products, arithmetic and copies ran while one was open for 0% of the time, Pallas kernels for 0%

profile of v4, /device:TPU:0, one launch (start us, length us, event | category | flops | bytes accessed | tf_op | source)
XLA Modules:
  0.0 102.0 jit_solution(1238871335546367913)
XLA Ops:
  0.0 0.0 copy-start.2
  0.0 0.0 copy-start.1
  0.0 4.6 %contributions.1 = bf16[8,16,72,128]{3,2,1,0:T(8,128)(2,1)} custom-call(s32[2,8]{1,0:T(2,128)} %bitcast.12, s32[2,8]{1,0:T(2,128)} %bitcast.13, bf16[8,128,128]{2,1,0:T(8,128)(2,1)} %velocity_hbm.1, bf16[8,2,2,256,128]{4,3,2,1,0:T(8,128)(2,1)} %coupling_hbm.1), custom_call_target="tpu_custom_call" | custom-call | tf_op jit(solution)/shard_map/contributions/pallas_call | solution.py:111
  4.6 0.0 copy-start
  4.6 43.5 %all_to_all.10.got_ref = bf16[128,72,128]{2,1,0:T(8,128)(2,1)S(1)} all-to-all(bf16[128,72,128]{2,1,0:T(8,128)(2,1)} %bitcast.11), channel_id=1, replica_groups=mesh['row'=8,'col'=16] {'row','col'}, dimensions={0} | all-to-all | bytes 4718592 | tf_op jit(solution)/shard_map/all_to_all | solution.py:284
  48.1 0.0 copy-done.2
  48.1 0.0 copy-start.3
  48.1 2.0 %cluster_sums.1 = (bf16[64,32,128]{2,1,0:T(8,128)(2,1)S(1)}, bf16[64,2,32,256]{3,2,1,0:T(8,128)(2,1)S(1)}) custom-call(bf16[128,72,128]{2,1,0:T(8,128)(2,1)S(1)} %all_to_all.10.got_ref, bf16[64,2,32,256]{3,2,1,0:T(8,128)(2,1)S(1)} %bitcast.9), custom_call_target="tpu_custom_call" | custom-call | tf_op jit(solution)/shard_map/cluster_sums/pallas_call | solution.py:159
  50.1 0.1 collective-permute-start.2
  50.2 0.7 collective-permute-start
  50.9 1.2 %collective-permute-done.2.refs_4_ = bf16[64,32,128]{2,1,0:T(8,128)(2,1)S(1)} collective-permute-done((bf16[64,32,128]{2,1,0:T(8,128)(2,1)S(1)}, bf16[64,32,128]{2,1,0:T(8,128)(2,1)S(1)}, u32[]{:S(2)}, u32[]{:S(2)}) %collective-permute-start.2) | collective-permute-done | bytes 524320 | tf_op jit(solution)/shard_map/ppermute | solution.py:181
  52.1 0.6 collective-permute-start.3
  52.8 7.9 %collective-permute-done.refs_1_ = bf16[64,32,128]{2,1,0:T(8,128)(2,1)S(1)} collective-permute-done((bf16[64,32,128]{2,1,0:T(8,128)(2,1)S(1)}, bf16[64,32,128]{2,1,0:T(8,128)(2,1)S(1)}, u32[]{:S(2)}, u32[]{:S(2)}) %collective-permute-start) | collective-permute-done | bytes 524320 | tf_op jit(solution)/shard_map/ppermute | solution.py:181
  60.7 0.0 collective-permute-start.1
  60.7 0.3 collective-permute-start.6
  61.0 5.3 %collective-permute-done.3.refs_5_ = bf16[64,32,128]{2,1,0:T(8,128)(2,1)S(1)} collective-permute-done((bf16[64,32,128]{2,1,0:T(8,128)(2,1)S(1)}, bf16[64,32,128]{2,1,0:T(8,128)(2,1)S(1)}, u32[]{:S(2)}, u32[]{:S(2)}) %collective-permute-start.3) | collective-permute-done | bytes 524320 | tf_op jit(solution)/shard_map/ppermute | solution.py:181
  66.3 0.0 collective-permute-start.4
  66.3 5.6 %collective-permute-done.1.refs_2_ = bf16[64,32,128]{2,1,0:T(8,128)(2,1)S(1)} collective-permute-done((bf16[64,32,128]{2,1,0:T(8,128)(2,1)S(1)}, bf16[64,32,128]{2,1,0:T(8,128)(2,1)S(1)}, u32[]{:S(2)}, u32[]{:S(2)}) %collective-permute-start.1) | collective-permute-done | bytes 524320 | tf_op jit(solution)/shard_map/ppermute | solution.py:181
  71.9 0.0 collective-permute-start.5
  71.9 0.0 collective-permute-done.6.refs_7_
  71.9 0.0 collective-permute-done.4.refs_3_
  71.9 1.9 %collective-permute-done.5.refs_6_ = bf16[64,32,128]{2,1,0:T(8,128)(2,1)S(1)} collective-permute-done((bf16[64,32,128]{2,1,0:T(8,128)(2,1)S(1)}, bf16[64,32,128]{2,1,0:T(8,128)(2,1)S(1)}, u32[]{:S(2)}, u32[]{:S(2)}) %collective-permute-start.5) | collective-permute-done | bytes 524320 | tf_op jit(solution)/shard_map/ppermute | solution.py:181
  73.8 0.0 copy-done.1
  73.8 0.0 copy-done
  73.8 0.0 copy-done.3
  73.9 6.2 %operator.1 = bf16[16,128,256]{2,1,0:T(8,128)(2,1)S(1)} custom-call(s32[96]{0:T(128)S(1)} %bitcast.10, bf16[64,32,128]{2,1,0:T(8,128)(2,1)S(1)} %get-tuple-element.7.refs_0_, bf16[64,32,128]{2,1,0:T(8,128)(2,1)S(1)} %collective-permute-done.refs_1_, bf16[64,32,128]{2,1,0:T(8,128)(2,1)S(1)} %collective-permute-done.1.refs_2_, ...), custom_call_target="tpu_custom_call" | custom-call | tf_op jit(solution)/shard_map/operator/pallas_call | solution.py:242
  80.1 21.0 %all_to_all.11.got_ref = bf16[16,128,256]{2,1,0:T(8,128)(2,1)S(1)} all-to-all(bf16[16,128,256]{2,1,0:T(8,128)(2,1)S(1)} %operator.1), channel_id=1, replica_groups=mesh['row'=8,'col'=16] {'col'}, dimensions={0} | all-to-all | bytes 2097152 | tf_op jit(solution)/shard_map/all_to_all | solution.py:288
  101.1 0.9 response_sum.1
Async XLA Ops:
  0.0 48.1 %copy-start.2 = (bf16[1,1,64,2,32,256]{5,4,3,2,1,0:T(8,128)(2,1)S(1)}, bf16[1,1,64,2,32,256]{5,4,3,2,1,0:T(8,128)(2,1)}, u32[]{:S(2)}) copy-start(bf16[1,1,64,2,32,256]{5,4,3,2,1,0:T(8,128)(2,1)} %param.14) | copy-start | bytes 6291460
  0.0 73.8 %copy-start.1 = (bf16[1,1,64,2,32,256]{5,4,3,2,1,0:T(8,128)(2,1)S(1)}, bf16[1,1,64,2,32,256]{5,4,3,2,1,0:T(8,128)(2,1)}, u32[]{:S(2)}) copy-start(bf16[1,1,64,2,32,256]{5,4,3,2,1,0:T(8,128)(2,1)} %param.13) | copy-start | bytes 6291460
  4.6 69.2 %copy-start = (bf16[1,1,32,2,256,256]{5,4,3,2,1,0:T(8,128)(2,1)S(1)}, bf16[1,1,32,2,256,256]{5,4,3,2,1,0:T(8,128)(2,1)}, u32[]{:S(2)}) copy-start(bf16[1,1,32,2,256,256]{5,4,3,2,1,0:T(8,128)(2,1)} %param.12) | copy-start | bytes 25165828
  48.1 25.7 %copy-start.3 = (s32[1,1,96]{2,1,0:T(1,128)S(1)}, s32[1,1,96]{2,1,0:T(1,128)}, u32[]{:S(2)}) copy-start(s32[1,1,96]{2,1,0:T(1,128)} %param.15) | copy-start | bytes 1156
  50.1 2.0 %collective-permute-start.2 = (bf16[64,32,128]{2,1,0:T(8,128)(2,1)S(1)}, bf16[64,32,128]{2,1,0:T(8,128)(2,1)S(1)}, u32[]{:S(2)}, u32[]{:S(2)}) collective-permute-start(bf16[64,32,128]{2,1,0:T(8,128)(2,1)S(1)} %get-tuple-element.7.refs_0_), channel_id=1, source_target_pairs={{0,16},{16,0},{32,48},{48,32},{64,80},{80,64},{96,112},{112,96},{1... | collective-permute-start | bytes 1572872 | tf_op jit(solution)/shard_map/ppermute | solution.py:181
  50.2 10.5 %collective-permute-start = (bf16[64,32,128]{2,1,0:T(8,128)(2,1)S(1)}, bf16[64,32,128]{2,1,0:T(8,128)(2,1)S(1)}, u32[]{:S(2)}, u32[]{:S(2)}) collective-permute-start(bf16[64,32,128]{2,1,0:T(8,128)(2,1)S(1)} %get-tuple-element.7.refs_0_), channel_id=1, source_target_pairs={{0,32},{16,112},{32,64},{48,16},{64,96},{80,48},{96,0},{112,80},{1... | collective-permute-start | bytes 1572872 | tf_op jit(solution)/shard_map/ppermute | solution.py:181
  52.1 14.2 %collective-permute-start.3 = (bf16[64,32,128]{2,1,0:T(8,128)(2,1)S(1)}, bf16[64,32,128]{2,1,0:T(8,128)(2,1)S(1)}, u32[]{:S(2)}, u32[]{:S(2)}) collective-permute-start(bf16[64,32,128]{2,1,0:T(8,128)(2,1)S(1)} %collective-permute-done.2.refs_4_), channel_id=1, source_target_pairs={{0,32},{16,112},{32,64},{48,16},{64,96},{80,48},{96,0},{112,80},{1... | collective-permute-start | bytes 1572872 | tf_op jit(solution)/shard_map/ppermute | solution.py:181
  60.7 11.2 %collective-permute-start.1 = (bf16[64,32,128]{2,1,0:T(8,128)(2,1)S(1)}, bf16[64,32,128]{2,1,0:T(8,128)(2,1)S(1)}, u32[]{:S(2)}, u32[]{:S(2)}) collective-permute-start(bf16[64,32,128]{2,1,0:T(8,128)(2,1)S(1)} %collective-permute-done.refs_1_), channel_id=1, source_target_pairs={{0,32},{16,112},{32,64},{48,16},{64,96},{80,48},{96,0},{112,80},{1... | collective-permute-start | bytes 1572872 | tf_op jit(solution)/shard_map/ppermute | solution.py:181
  60.7 11.2 %collective-permute-start.6 = (bf16[64,32,128]{2,1,0:T(8,128)(2,1)S(1)}, bf16[64,32,128]{2,1,0:T(8,128)(2,1)S(1)}, u32[]{:S(2)}, u32[]{:S(2)}) collective-permute-start(bf16[64,32,128]{2,1,0:T(8,128)(2,1)S(1)} %collective-permute-done.refs_1_), channel_id=1, source_target_pairs={{0,16},{16,0},{32,48},{48,32},{64,80},{80,64},{96,112},{112,96},{1... | collective-permute-start | bytes 1572872 | tf_op jit(solution)/shard_map/ppermute | solution.py:181
  66.3 5.6 %collective-permute-start.4 = (bf16[64,32,128]{2,1,0:T(8,128)(2,1)S(1)}, bf16[64,32,128]{2,1,0:T(8,128)(2,1)S(1)}, u32[]{:S(2)}, u32[]{:S(2)}) collective-permute-start(bf16[64,32,128]{2,1,0:T(8,128)(2,1)S(1)} %collective-permute-done.3.refs_5_), channel_id=1, source_target_pairs={{0,16},{16,0},{32,48},{48,32},{64,80},{80,64},{96,112},{112,96},{1... | collective-permute-start | bytes 1572872 | tf_op jit(solution)/shard_map/ppermute | solution.py:181
  71.9 1.9 %collective-permute-start.5 = (bf16[64,32,128]{2,1,0:T(8,128)(2,1)S(1)}, bf16[64,32,128]{2,1,0:T(8,128)(2,1)S(1)}, u32[]{:S(2)}, u32[]{:S(2)}) collective-permute-start(bf16[64,32,128]{2,1,0:T(8,128)(2,1)S(1)} %collective-permute-done.1.refs_2_), channel_id=1, source_target_pairs={{0,16},{16,0},{32,48},{48,32},{64,80},{80,64},{96,112},{112,96},{1... | collective-permute-start | bytes 1572872 | tf_op jit(solution)/shard_map/ppermute | solution.py:181

commit v5 on v4

--- a/solution.py
+++ b/solution.py
@@ -127,7 +127,8 @@
     )(dest.T, cluster.T, velocity, coupling)
 
 
-def cluster_kernel(got_ref, block_hbm, out_ref, block_ref, total_ref, other_ref, ids_vec_ref, ids_ref, sem, block_sem):
+def cluster_kernel(got_ref, block_hbm, out_ref, block_ref, *refs):
+    totals, (ids_vec_ref, ids_ref, sem, block_sem) = refs[:4], refs[4:]
     block_copy = pltpu.make_async_copy(block_hbm, block_ref, block_sem)
     block_copy.start()
     devices = got_ref.shape[0]
@@ -137,21 +138,21 @@
     ids_vec_ref[...] = ids.astype(jnp.int32)
     copy = pltpu.make_async_copy(ids_vec_ref, ids_ref, sem)
     copy.start()
-    total_ref[...] = jnp.zeros_like(total_ref)
-    other_ref[...] = jnp.zeros_like(other_ref)
+    for sums_ref in totals:
+        sums_ref[...] = jnp.zeros_like(sums_ref)
     copy.wait()
 
-    for row in range(devices // 64):
-
-        def add(i, carry):
-            for slot, sums_ref in enumerate((total_ref, other_ref)):
-                k = ids_ref[row, 2 * i + slot]
-                piece = got_ref[row * 64 + i, slot * 2 * PIECE : (slot + 1) * 2 * PIECE, :]
-                sums_ref[k] = sums_ref[k] + piece.astype(F32)
-            return carry
-
-        lax.fori_loop(0, 64, add, 0, unroll=8)
-    out_ref[...] = (total_ref[:CLUSTERS] + other_ref[:CLUSTERS]).astype(BF16)
+    def add(i, carry):
+        for j, sums_ref in enumerate(totals):
+            row, slot = j // SLOTS, j % SLOTS
+            k = ids_ref[row, 2 * i + slot]
+            piece = got_ref[row * 64 + i, slot * 2 * PIECE : (slot + 1) * 2 * PIECE, :]
+            sums_ref[k] = sums_ref[k] + piece.astype(F32)
+        return carry
+
+    lax.fori_loop(0, 64, add, 0, unroll=4)
+    sums = [sums_ref[:CLUSTERS] for sums_ref in totals]
+    out_ref[...] = ((sums[0] + sums[1]) + (sums[2] + sums[3])).astype(BF16)
     block_copy.wait()
 
 
@@ -165,6 +166,8 @@
         in_specs=[pl.BlockSpec(memory_space=pltpu.VMEM), pl.BlockSpec(memory_space=pltpu.HBM)],
         out_specs=[pl.BlockSpec(memory_space=pltpu.VMEM)] * 2,
         scratch_shapes=[
+            pltpu.VMEM((CLUSTERS + 1, 2 * PIECE, 128), F32),
+            pltpu.VMEM((CLUSTERS + 1, 2 * PIECE, 128), F32),
             pltpu.VMEM((CLUSTERS + 1, 2 * PIECE, 128), F32),
             pltpu.VMEM((CLUSTERS + 1, 2 * PIECE, 128), F32),
             pltpu.VMEM((8, 128), jnp.int32),

time: 102 us -> 102 us (level)
  no operation moved by 1% of the time
where the time goes in v5:
time: 102 us
  blocking collectives  64.5 us (63%)
  waiting for transfers between devices  22 us (22%)
  Pallas kernels  13.6 us (13%)
  starting transfers between devices  1.69 us (2%)
    all_to_all x1, blocking collectives, per_device(): lax.all_to_all(messages, ('row', 'col'), split_axis=0, concat_axis=0, til...  43.5 us
    ppermute x7, waiting for transfers between devices, shift_rows(): return lax.ppermute(values, 'row', pairs)  22 us
    all_to_all x1, blocking collectives, per_device(): lax.all_to_all(partial, 'col', split_axis=0, concat_axis=0, tiled=True)  21 us
    pallas_call x1, Pallas kernels, apply_operator(): pl.pallas_call(operator_kernel, out_shape=jax.ShapeDtypeStruct((COLS, WID...  6.25 us
    pallas_call x1, Pallas kernels, contributions(): pl.pallas_call(contribution_kernel, out_shape=jax.ShapeDtypeStruct((ROWS,...  4.61 us
  transfers between devices with their start and end apart: 7, of which 5 were waited for; matrix products, arithmetic and copies ran while one was open for 0% of the time, Pallas kernels for 0%

profile of v5, /device:TPU:0, one launch (start us, length us, event | category | flops | bytes accessed | tf_op | source)
XLA Modules:
  0.0 101.9 jit_solution(12246851884402789864)
XLA Ops:
  0.0 0.0 copy-start.2
  0.0 0.0 copy-start.1
  0.0 4.6 %contributions.1 = bf16[8,16,72,128]{3,2,1,0:T(8,128)(2,1)} custom-call(s32[2,8]{1,0:T(2,128)} %bitcast.12, s32[2,8]{1,0:T(2,128)} %bitcast.13, bf16[8,128,128]{2,1,0:T(8,128)(2,1)} %velocity_hbm.1, bf16[8,2,2,256,128]{4,3,2,1,0:T(8,128)(2,1)} %coupling_hbm.1), custom_call_target="tpu_custom_call" | custom-call | tf_op jit(solution)/shard_map/contributions/pallas_call | solution.py:111
  4.6 0.0 copy-start
  4.6 43.5 %all_to_all.10.got_ref = bf16[128,72,128]{2,1,0:T(8,128)(2,1)S(1)} all-to-all(bf16[128,72,128]{2,1,0:T(8,128)(2,1)} %bitcast.11), channel_id=1, replica_groups=mesh['row'=8,'col'=16] {'row','col'}, dimensions={0} | all-to-all | bytes 4718592 | tf_op jit(solution)/shard_map/all_to_all | solution.py:287
  48.1 0.0 copy-done.2
  48.1 0.0 copy-start.3
  48.1 1.9 %cluster_sums.1 = (bf16[64,32,128]{2,1,0:T(8,128)(2,1)S(1)}, bf16[64,2,32,256]{3,2,1,0:T(8,128)(2,1)S(1)}) custom-call(bf16[128,72,128]{2,1,0:T(8,128)(2,1)S(1)} %all_to_all.10.got_ref, bf16[64,2,32,256]{3,2,1,0:T(8,128)(2,1)S(1)} %bitcast.9), custom_call_target="tpu_custom_call" | custom-call | tf_op jit(solution)/shard_map/cluster_sums/pallas_call | solution.py:160
  50.0 0.1 collective-permute-start.2
  50.1 0.7 collective-permute-start
  50.8 1.2 %collective-permute-done.2.refs_4_ = bf16[64,32,128]{2,1,0:T(8,128)(2,1)S(1)} collective-permute-done((bf16[64,32,128]{2,1,0:T(8,128)(2,1)S(1)}, bf16[64,32,128]{2,1,0:T(8,128)(2,1)S(1)}, u32[]{:S(2)}, u32[]{:S(2)}) %collective-permute-start.2) | collective-permute-done | bytes 524320 | tf_op jit(solution)/shard_map/ppermute | solution.py:184
  52.0 0.6 collective-permute-start.3
  52.6 7.9 %collective-permute-done.refs_1_ = bf16[64,32,128]{2,1,0:T(8,128)(2,1)S(1)} collective-permute-done((bf16[64,32,128]{2,1,0:T(8,128)(2,1)S(1)}, bf16[64,32,128]{2,1,0:T(8,128)(2,1)S(1)}, u32[]{:S(2)}, u32[]{:S(2)}) %collective-permute-start) | collective-permute-done | bytes 524320 | tf_op jit(solution)/shard_map/ppermute | solution.py:184
  60.6 0.0 collective-permute-start.1
  60.6 0.3 collective-permute-start.6
  60.8 5.3 %collective-permute-done.3.refs_5_ = bf16[64,32,128]{2,1,0:T(8,128)(2,1)S(1)} collective-permute-done((bf16[64,32,128]{2,1,0:T(8,128)(2,1)S(1)}, bf16[64,32,128]{2,1,0:T(8,128)(2,1)S(1)}, u32[]{:S(2)}, u32[]{:S(2)}) %collective-permute-start.3) | collective-permute-done | bytes 524320 | tf_op jit(solution)/shard_map/ppermute | solution.py:184
  66.2 0.0 collective-permute-start.4
  66.2 5.6 %collective-permute-done.1.refs_2_ = bf16[64,32,128]{2,1,0:T(8,128)(2,1)S(1)} collective-permute-done((bf16[64,32,128]{2,1,0:T(8,128)(2,1)S(1)}, bf16[64,32,128]{2,1,0:T(8,128)(2,1)S(1)}, u32[]{:S(2)}, u32[]{:S(2)}) %collective-permute-start.1) | collective-permute-done | bytes 524320 | tf_op jit(solution)/shard_map/ppermute | solution.py:184
  71.8 0.0 collective-permute-start.5
  71.8 0.0 collective-permute-done.6.refs_7_
  71.8 0.0 collective-permute-done.4.refs_3_
  71.8 1.9 %collective-permute-done.5.refs_6_ = bf16[64,32,128]{2,1,0:T(8,128)(2,1)S(1)} collective-permute-done((bf16[64,32,128]{2,1,0:T(8,128)(2,1)S(1)}, bf16[64,32,128]{2,1,0:T(8,128)(2,1)S(1)}, u32[]{:S(2)}, u32[]{:S(2)}) %collective-permute-start.5) | collective-permute-done | bytes 524320 | tf_op jit(solution)/shard_map/ppermute | solution.py:184
  73.7 0.0 copy-done.1
  73.7 0.0 copy-done
  73.7 0.0 copy-done.3
  73.7 6.2 %operator.1 = bf16[16,128,256]{2,1,0:T(8,128)(2,1)S(1)} custom-call(s32[96]{0:T(128)S(1)} %bitcast.10, bf16[64,32,128]{2,1,0:T(8,128)(2,1)S(1)} %get-tuple-element.7.refs_0_, bf16[64,32,128]{2,1,0:T(8,128)(2,1)S(1)} %collective-permute-done.refs_1_, bf16[64,32,128]{2,1,0:T(8,128)(2,1)S(1)} %collective-permute-done.1.refs_2_, ...), custom_call_target="tpu_custom_call" | custom-call | tf_op jit(solution)/shard_map/operator/pallas_call | solution.py:245
  80.0 21.0 %all_to_all.11.got_ref = bf16[16,128,256]{2,1,0:T(8,128)(2,1)S(1)} all-to-all(bf16[16,128,256]{2,1,0:T(8,128)(2,1)S(1)} %operator.1), channel_id=1, replica_groups=mesh['row'=8,'col'=16] {'col'}, dimensions={0} | all-to-all | bytes 2097152 | tf_op jit(solution)/shard_map/all_to_all | solution.py:291
  101.0 0.9 response_sum.1
Async XLA Ops:
  0.0 48.1 %copy-start.2 = (bf16[1,1,64,2,32,256]{5,4,3,2,1,0:T(8,128)(2,1)S(1)}, bf16[1,1,64,2,32,256]{5,4,3,2,1,0:T(8,128)(2,1)}, u32[]{:S(2)}) copy-start(bf16[1,1,64,2,32,256]{5,4,3,2,1,0:T(8,128)(2,1)} %param.14) | copy-start | bytes 6291460
  0.0 73.7 %copy-start.1 = (bf16[1,1,64,2,32,256]{5,4,3,2,1,0:T(8,128)(2,1)S(1)}, bf16[1,1,64,2,32,256]{5,4,3,2,1,0:T(8,128)(2,1)}, u32[]{:S(2)}) copy-start(bf16[1,1,64,2,32,256]{5,4,3,2,1,0:T(8,128)(2,1)} %param.13) | copy-start | bytes 6291460
  4.6 69.1 %copy-start = (bf16[1,1,32,2,256,256]{5,4,3,2,1,0:T(8,128)(2,1)S(1)}, bf16[1,1,32,2,256,256]{5,4,3,2,1,0:T(8,128)(2,1)}, u32[]{:S(2)}) copy-start(bf16[1,1,32,2,256,256]{5,4,3,2,1,0:T(8,128)(2,1)} %param.12) | copy-start | bytes 25165828
  48.1 25.6 %copy-start.3 = (s32[1,1,96]{2,1,0:T(1,128)S(1)}, s32[1,1,96]{2,1,0:T(1,128)}, u32[]{:S(2)}) copy-start(s32[1,1,96]{2,1,0:T(1,128)} %param.15) | copy-start | bytes 1156
  50.0 2.0 %collective-permute-start.2 = (bf16[64,32,128]{2,1,0:T(8,128)(2,1)S(1)}, bf16[64,32,128]{2,1,0:T(8,128)(2,1)S(1)}, u32[]{:S(2)}, u32[]{:S(2)}) collective-permute-start(bf16[64,32,128]{2,1,0:T(8,128)(2,1)S(1)} %get-tuple-element.7.refs_0_), channel_id=1, source_target_pairs={{0,16},{16,0},{32,48},{48,32},{64,80},{80,64},{96,112},{112,96},{1... | collective-permute-start | bytes 1572872 | tf_op jit(solution)/shard_map/ppermute | solution.py:184
  50.1 10.5 %collective-permute-start = (bf16[64,32,128]{2,1,0:T(8,128)(2,1)S(1)}, bf16[64,32,128]{2,1,0:T(8,128)(2,1)S(1)}, u32[]{:S(2)}, u32[]{:S(2)}) collective-permute-start(bf16[64,32,128]{2,1,0:T(8,128)(2,1)S(1)} %get-tuple-element.7.refs_0_), channel_id=1, source_target_pairs={{0,32},{16,112},{32,64},{48,16},{64,96},{80,48},{96,0},{112,80},{1... | collective-permute-start | bytes 1572872 | tf_op jit(solution)/shard_map/ppermute | solution.py:184
  52.0 14.2 %collective-permute-start.3 = (bf16[64,32,128]{2,1,0:T(8,128)(2,1)S(1)}, bf16[64,32,128]{2,1,0:T(8,128)(2,1)S(1)}, u32[]{:S(2)}, u32[]{:S(2)}) collective-permute-start(bf16[64,32,128]{2,1,0:T(8,128)(2,1)S(1)} %collective-permute-done.2.refs_4_), channel_id=1, source_target_pairs={{0,32},{16,112},{32,64},{48,16},{64,96},{80,48},{96,0},{112,80},{1... | collective-permute-start | bytes 1572872 | tf_op jit(solution)/shard_map/ppermute | solution.py:184
  60.6 11.2 %collective-permute-start.1 = (bf16[64,32,128]{2,1,0:T(8,128)(2,1)S(1)}, bf16[64,32,128]{2,1,0:T(8,128)(2,1)S(1)}, u32[]{:S(2)}, u32[]{:S(2)}) collective-permute-start(bf16[64,32,128]{2,1,0:T(8,128)(2,1)S(1)} %collective-permute-done.refs_1_), channel_id=1, source_target_pairs={{0,32},{16,112},{32,64},{48,16},{64,96},{80,48},{96,0},{112,80},{1... | collective-permute-start | bytes 1572872 | tf_op jit(solution)/shard_map/ppermute | solution.py:184
  60.6 11.2 %collective-permute-start.6 = (bf16[64,32,128]{2,1,0:T(8,128)(2,1)S(1)}, bf16[64,32,128]{2,1,0:T(8,128)(2,1)S(1)}, u32[]{:S(2)}, u32[]{:S(2)}) collective-permute-start(bf16[64,32,128]{2,1,0:T(8,128)(2,1)S(1)} %collective-permute-done.refs_1_), channel_id=1, source_target_pairs={{0,16},{16,0},{32,48},{48,32},{64,80},{80,64},{96,112},{112,96},{1... | collective-permute-start | bytes 1572872 | tf_op jit(solution)/shard_map/ppermute | solution.py:184
  66.2 5.6 %collective-permute-start.4 = (bf16[64,32,128]{2,1,0:T(8,128)(2,1)S(1)}, bf16[64,32,128]{2,1,0:T(8,128)(2,1)S(1)}, u32[]{:S(2)}, u32[]{:S(2)}) collective-permute-start(bf16[64,32,128]{2,1,0:T(8,128)(2,1)S(1)} %collective-permute-done.3.refs_5_), channel_id=1, source_target_pairs={{0,16},{16,0},{32,48},{48,32},{64,80},{80,64},{96,112},{112,96},{1... | collective-permute-start | bytes 1572872 | tf_op jit(solution)/shard_map/ppermute | solution.py:184
  71.8 1.9 %collective-permute-start.5 = (bf16[64,32,128]{2,1,0:T(8,128)(2,1)S(1)}, bf16[64,32,128]{2,1,0:T(8,128)(2,1)S(1)}, u32[]{:S(2)}, u32[]{:S(2)}) collective-permute-start(bf16[64,32,128]{2,1,0:T(8,128)(2,1)S(1)} %collective-permute-done.1.refs_2_), channel_id=1, source_target_pairs={{0,16},{16,0},{32,48},{48,32},{64,80},{80,64},{96,112},{112,96},{1... | collective-permute-start | bytes 1572872 | tf_op jit(solution)/shard_map/ppermute | solution.py:184
